TPU v7x, 1024 devices: a whole 8x8x8 slice. The times are simulated.
1024 devices in a mesh: fsdp: 64 (over z, x), expert: 4 (over y_lo), dp: 4 (over y_hi, core).
Axes of the slice: x: 8, y: 8 (y_hi: 2, y_lo: 4; y = y_hi * 4 + y_lo), z: 8, core: 2. Of those that a mesh axis runs over, the one named last changes fastest.
Arguments:
- tokens: bfloat16 [128, 16, 2048], P('fsdp', ('expert', 'dp')), may hold values from -6 to 6
- cotangent: bfloat16 [128, 16, 2048], P('fsdp', ('expert', 'dp')), may hold values from -4 to 4
- expert_ids: int32 [128, 16, 2], P(None, ('expert', 'dp')), may hold values from 0 to 3, as said below
- slot_ids: int32 [128, 16, 2], P(None, ('expert', 'dp')), may hold values from -1 to 63, as said below
- route_probs: bfloat16 [128, 16, 2], P(None, ('expert', 'dp')), may hold values from 0.049804688 to 0.94921875
- gate_weight: bfloat16 [4, 2048, 8192], P('expert', None, 'fsdp'), may hold values from -0.125 to 0.125
- up_weight: bfloat16 [4, 2048, 8192], P('expert', None, 'fsdp'), may hold values from -0.125 to 0.125
- down_weight: bfloat16 [4, 8192, 2048], P('expert', 'fsdp'), may hold values from -0.0625 to 0.0625
Outputs:
- grad_gate: bfloat16 [4, 2048, 8192], P('expert', 'dp', 'fsdp')
- grad_up: bfloat16 [4, 2048, 8192], P('expert', 'dp', 'fsdp')
- grad_down: bfloat16 [4, 8192, 2048], P('expert', 'fsdp', 'dp')
- token_grad: bfloat16 [128, 16, 2048], P('fsdp', ('expert', 'dp'))
- prob_grad: float32 [128, 16, 2], P('fsdp', ('expert', 'dp'))
Inputs may be any that keep to these rules, and one draw needn't show every extreme that they name: `expert_ids`: each token names two different experts. `slot_ids`: within a group, the choices of one expert get slots 0, 1, 2, ... by arrival in token order, a token's first choice before its second; a choice arriving after all 64 slots of its expert are taken gets -1 and is dropped. In every group some expert receives more than 64 choices, and it is the same expert in all groups of one dp index.
All inputs are finite; a program needn't handle non-finite values.
Results may differ from a plain program's by a relative error of at most 0.015.
Values may be sent and summed in bfloat16 or wider, within the bound.
No kernel may reach another device: no remote copies, remote signals or barrier semaphores. Data moves between devices by JAX's collectives and lax.ppermute only.
A program may use at most 32 MiB of HBM per device.

v0:
```python
import math

import jax
import jax.numpy as jnp
from jax import lax
from jax.sharding import PartitionSpec as P


def in_one_piece(arrays, axis, split_dim, concat_dim, along):
    widths = [math.prod(a.shape[along:]) for a in arrays]
    both = jnp.concatenate(
        [a.reshape(*a.shape[:along], w) for a, w in zip(arrays, widths)], axis=along
    )
    out = lax.all_to_all(both, axis, split_axis=split_dim, concat_axis=concat_dim, tiled=True)
    tiles = jnp.split(out, [sum(widths[:k]) for k in range(1, len(widths))], axis=along)
    return tuple((b.reshape(*out.shape[:along], *a.shape[along:]) for a, b in zip(arrays, tiles)))


def rows_first(arrays, axis, dims):
    turned = [jnp.moveaxis(a, dim, 0) for a, dim in zip(arrays, dims)]
    both = jnp.concatenate([t.reshape(len(t), -1) for t in turned], axis=1)
    out, at, outs = (lax.all_gather(both, axis, axis=0, tiled=True), 0, [])
    for t, dim in zip(turned, dims):
        share = out[:, at : at + t[0].size].reshape(-1, *t.shape[1:])
        outs.append(jnp.moveaxis(share, 0, dim))
        at += t[0].size
    return tuple(outs)


def side_by_side(arrays, axis, split_dim, concat_dim, along):
    ends, at = ([], 0)
    for a in arrays[:-1]:
        at += a.shape[along]
        ends.append(at)
    both = jnp.concatenate(arrays, axis=along)
    return tuple(
        jnp.split(
            lax.all_to_all(both, axis, split_axis=split_dim, concat_axis=concat_dim, tiled=True),
            ends,
            axis=along,
        )
    )


def sent_together(arrays, axis, dim, along):
    ends, at = ([], 0)
    for a in arrays[:-1]:
        at += a.shape[along]
        ends.append(at)
    both = jnp.concatenate(arrays, axis=along)
    return tuple(jnp.split(lax.all_gather(both, axis, axis=dim, tiled=True), ends, axis=along))


def in_blocks(value, dim, peers):
    before, after = (value.shape[:dim], value.shape[dim + 1 :])
    return jnp.moveaxis(value.reshape(*before, peers, -1, *after), dim, 0)


def sum_at_owner(value, axis, dim):
    peers = lax.axis_size(axis)
    tiles = lax.all_to_all(in_blocks(value, dim, peers), axis, 0, 0, tiled=True)
    return jnp.sum(tiles, axis=0)


def route_rows(group_ids, group_slots, local_count, peer_count, capacity):
    kept_slot = group_slots >= 0
    target = (
        group_ids % local_count * (peer_count * capacity)
        + group_ids // local_count * capacity
        + jnp.where(kept_slot, group_slots, 0)
    )
    total_rows = local_count * peer_count * capacity
    row_iota = lax.broadcasted_iota(jnp.int32, (total_rows, group_ids.shape[0]), 0)
    leading = jnp.logical_and(row_iota == target[None, :, 0], kept_slot[None, :, 0])
    trailing = jnp.logical_and(row_iota == target[None, :, 1], kept_slot[None, :, 1])
    return (leading, trailing)


def summed(values):
    return jnp.sum(
        lax.optimization_barrier(values.astype(jnp.bfloat16)).astype(jnp.float32), axis=1
    )


def shards(
    tokens, cotangent, expert_ids, slot_ids, route_probs, gate_weight, up_weight, down_weight
):
    local_experts = gate_weight.shape[0]
    model_width = tokens.shape[2]
    group_count = expert_ids.shape[0]
    peer_count = lax.axis_size("expert")
    capacity = 2 * group_count // (local_experts * peer_count)
    per_expert = peer_count * capacity
    total_rows = local_experts * per_expert
    leading, trailing = route_rows(
        expert_ids[:, 0, :], slot_ids[:, 0, :], local_experts, peer_count, capacity
    )
    either = jnp.logical_or(leading, trailing).astype(jnp.bfloat16)
    prob_pair = route_probs[:, 0, :].astype(jnp.float32)
    prob_rows = jnp.sum(
        jnp.where(leading, prob_pair[None, :, 0], 0.0)
        + jnp.where(trailing, prob_pair[None, :, 1], 0.0),
        axis=1,
    )
    prob_rows = prob_rows.astype(jnp.bfloat16).reshape(local_experts, peer_count, capacity)
    own_x = tokens[:, 0, :]
    own_dy = cotangent[:, 0, :]
    column_x, column_dy = (
        lax.all_to_all(own_x, "fsdp", split_axis=1, concat_axis=0, tiled=True),
        lax.all_to_all(own_dy, "fsdp", split_axis=1, concat_axis=0, tiled=True),
    )
    sent_x = (
        jnp.dot(either, column_x, preferred_element_type=jnp.float32)
        .astype(jnp.bfloat16)
        .reshape(local_experts, peer_count, capacity, -1)
    )
    sent_dy = (
        jnp.dot(either, column_dy, preferred_element_type=jnp.float32)
        .astype(jnp.bfloat16)
        .reshape(local_experts, peer_count, capacity, -1)
    )
    recv_x, recv_dy, recv_prob = in_one_piece((sent_x, sent_dy, prob_rows), "expert", 1, 1, 3)
    recv_x, recv_dy = rows_first((recv_x, recv_dy), "fsdp", (3, 3))
    rows_x = recv_x.reshape(local_experts, per_expert, model_width)
    rows_dy = recv_dy.reshape(local_experts, per_expert, model_width)
    prob_column = recv_prob.reshape(local_experts, per_expert, 1).astype(jnp.float32)
    gate_value = jnp.einsum("erd,edh->erh", rows_x, gate_weight, preferred_element_type=jnp.float32)
    up_value = jnp.einsum("erd,edh->erh", rows_x, up_weight, preferred_element_type=jnp.float32)
    back_value = jnp.einsum(
        "erd,ehd->erh", rows_dy, down_weight, preferred_element_type=jnp.float32
    )
    sigmoid_gate = jax.nn.sigmoid(gate_value)
    swish_gate = gate_value * sigmoid_gate
    hidden_full = swish_gate * up_value
    hidden = hidden_full.astype(jnp.bfloat16)
    scaled = (prob_column * hidden_full).astype(jnp.bfloat16)
    row_score = jnp.sum(hidden.astype(jnp.float32) * back_value, axis=2)
    back_scaled = prob_column * back_value
    grad_pre = (
        back_scaled * up_value * sigmoid_gate * (1.0 + gate_value * (1.0 - sigmoid_gate))
    ).astype(jnp.bfloat16)
    grad_upper = (back_scaled * swish_gate).astype(jnp.bfloat16)
    slot_dx = jnp.einsum(
        "erh,edh->erd", grad_pre, gate_weight, preferred_element_type=jnp.float32
    ) + jnp.einsum("erh,edh->erd", grad_upper, up_weight, preferred_element_type=jnp.float32)
    replica_count = lax.axis_size("dp")
    far_x, far_dy = side_by_side((rows_x, rows_dy), "dp", 2, 1, 0)
    far_pre, far_upper, far_scaled = sent_together((grad_pre, grad_upper, scaled), "dp", 1, 0)
    quarter = far_x.shape[2]
    hidden_count = far_pre.shape[2]
    far_x = far_x.reshape(local_experts, replica_count, per_expert, quarter)
    far_dy = far_dy.reshape(local_experts, replica_count, per_expert, quarter)
    far_pre = far_pre.reshape(local_experts, replica_count, per_expert, hidden_count)
    far_upper = far_upper.reshape(local_experts, replica_count, per_expert, hidden_count)
    far_scaled = far_scaled.reshape(local_experts, replica_count, per_expert, hidden_count)
    grad_gate = summed(
        jnp.einsum("esrd,esrh->esdh", far_x, far_pre, preferred_element_type=jnp.float32)
    )
    grad_up = summed(
        jnp.einsum("esrd,esrh->esdh", far_x, far_upper, preferred_element_type=jnp.float32)
    )
    grad_down = summed(
        jnp.einsum("esrh,esrd->eshd", far_scaled, far_dy, preferred_element_type=jnp.float32)
    )
    back_dx, back_score = tuple(
        (
            part.astype(jnp.float32)
            for part in in_one_piece(
                (
                    slot_dx.reshape(local_experts, peer_count, capacity, model_width).astype(
                        jnp.bfloat16
                    ),
                    row_score.reshape(local_experts, peer_count, capacity).astype(jnp.bfloat16),
                ),
                "expert",
                1,
                1,
                3,
            )
        )
    )
    flat_dx = back_dx.reshape(total_rows, model_width)
    flat_score = back_score.reshape(total_rows)
    leading_f = leading.astype(jnp.float32)
    trailing_f = trailing.astype(jnp.float32)
    group_dx = lax.dot_general(
        leading_f + trailing_f, flat_dx, (((0,), (0,)), ((), ())), precision=lax.Precision.HIGHEST
    )
    group_prob = jnp.stack(
        [
            jnp.dot(flat_score, leading_f, precision=lax.Precision.HIGHEST),
            jnp.dot(flat_score, trailing_f, precision=lax.Precision.HIGHEST),
        ],
        axis=1,
    )
    token_dx, token_prob = (sum_at_owner(group_dx, "fsdp", 0), sum_at_owner(group_prob, "fsdp", 0))
    return (
        grad_gate.astype(jnp.bfloat16),
        grad_up.astype(jnp.bfloat16),
        grad_down.astype(jnp.bfloat16),
        token_dx.astype(jnp.bfloat16)[:, None, :],
        token_prob[:, None, :],
    )


def solution(mesh):
    return jax.shard_map(
        shards,
        mesh=mesh,
        in_specs=(
            P("fsdp", ("expert", "dp"), None),
            P("fsdp", ("expert", "dp"), None),
            P(None, ("expert", "dp"), None),
            P(None, ("expert", "dp"), None),
            P(None, ("expert", "dp"), None),
            P("expert", None, "fsdp"),
            P("expert", None, "fsdp"),
            P("expert", "fsdp", None),
        ),
        out_specs=(
            P("expert", "dp", "fsdp"),
            P("expert", "dp", "fsdp"),
            P("expert", "fsdp", "dp"),
            P("fsdp", ("expert", "dp"), None),
            P("fsdp", ("expert", "dp"), None),
        ),
        check_vma=False,
    )
```

profile of v0, /device:TPU:2, one launch (start us, length us, event | category | flops | bytes accessed | tf_op | source)
XLA Modules:
  0.0 315.1 jit_solution(11809931979854608531)
XLA Ops:
  7.2 0.8 all_to_all.55
  8.0 0.7 copy.90
  8.7 22.7 %all-to-all-start.1 = ((bf16[2,64,32]{2,0,1:T(2,128)(2,1)}), bf16[2,64,32]{2,0,1:T(2,128)(2,1)S(1)}, u32[]{:S(2)}, u32[]{:S(2)}) async-start(bf16[2,64,32]{2,0,1:T(2,128)(2,1)} %copy.90), calls=%async_computation.1 | async-start | bytes 65536 | tf_op jit(solution)/shard_map/all_to_all | solution.py:110
  31.4 0.7 bitcast_convert_fusion
  32.0 0.7 bitcast_compare_fusion
  32.7 0.7 fusion.47
  33.9 0.8 all_to_all.51
  34.6 0.7 copy.89
  35.3 7.0 %all-to-all-done.1 = bf16[2,64,32]{2,0,1:T(2,128)(2,1)S(1)} async-done(((bf16[2,64,32]{2,0,1:T(2,128)(2,1)}), bf16[2,64,32]{2,0,1:T(2,128)(2,1)S(1)}, u32[]{:S(2)}, u32[]{:S(2)}) %all-to-all-start.1) | async-done | bytes 8224 | tf_op jit(solution)/shard_map/all_to_all | solution.py:110
  42.3 5.7 %all-to-all-start = ((bf16[2,64,32]{2,0,1:T(2,128)(2,1)}), bf16[2,64,32]{2,0,1:T(2,128)(2,1)S(1)}, u32[]{:S(2)}, u32[]{:S(2)}) async-start(bf16[2,64,32]{2,0,1:T(2,128)(2,1)} %copy.89), calls=%async_computation | async-start | bytes 65536 | tf_op jit(solution)/shard_map/all_to_all | solution.py:109
  48.4 10.6 %all-to-all-done = bf16[2,64,32]{2,0,1:T(2,128)(2,1)S(1)} async-done(((bf16[2,64,32]{2,0,1:T(2,128)(2,1)}), bf16[2,64,32]{2,0,1:T(2,128)(2,1)S(1)}, u32[]{:S(2)}, u32[]{:S(2)}) %all-to-all-start) | async-done | bytes 8224 | tf_op jit(solution)/shard_map/all_to_all | solution.py:109
  59.4 10.8 %all_to_all.73 = bf16[1,4,64,65]{3,2,0,1:T(8,128)(2,1)S(1)} all-to-all(bf16[1,4,64,65]{3,2,0,1:T(8,128)(2,1)S(1)} %pad_maximum_fusion.3), channel_id=1, replica_groups=mesh['fsdp'=64,'expert'=4,'dp'=4] {'expert'}, dimensions={1} | all-to-all | bytes 66560 | tf_op jit(solution)/shard_map/all_to_all | solution.py:14
  70.4 0.6 pad_maximum_fusion.4
  71.3 80.2 %all-gather.2.cloned.1.call-done = bf16[2048,512]{1,0:T(8,128)(2,1)} async-done(((bf16[32,512]{1,0:T(8,128)(2,1)}), bf16[2048,512]{1,0:T(8,128)(2,1)}) %all-gather.2.cloned.1.call-update) | async-done | bytes 2097168 | tf_op jit(solution)/shard_map/all_gather | solution.py:22
  151.6 2.7 fusion.48
  154.2 0.6 copy.125
  154.9 1.5 copy.126
  156.4 1.5 fusion.4
  158.0 0.5 fusion.6
  158.5 0.5 multiply_reduce_fusion
  159.3 0.5 fusion.10
  159.7 0.5 fusion
  160.2 1.1 pad_maximum_fusion.1
  161.3 4.7 %all-to-all-start.4 = ((bf16[1,4,64,2049]{3,2,0,1:T(8,128)(2,1)}), bf16[1,4,64,2049]{3,2,0,1:T(8,128)(2,1)}, u32[]{:S(2)}, u32[]{:S(2)}) async-start(bf16[1,4,64,2049]{3,2,0,1:T(8,128)(2,1)} %pad_maximum_fusion.1), calls=%async_computation.4 | async-start | bytes 2228224 | tf_op jit(solution)/shard_map/all_to_all | solution.py:14
  166.9 22.6 %all-to-all-done.4 = bf16[1,4,64,2049]{3,2,0,1:T(8,128)(2,1)} async-done(((bf16[1,4,64,2049]{3,2,0,1:T(8,128)(2,1)}), bf16[1,4,64,2049]{3,2,0,1:T(8,128)(2,1)}, u32[]{:S(2)}, u32[]{:S(2)}) %all-to-all-start.4) | async-done | bytes 1049120 | tf_op jit(solution)/shard_map/all_to_all | solution.py:14
  189.5 0.9 slice_reduce_fusion
  191.0 0.8 copy.111
  191.8 8.8 %all-to-all-start.6 = ((f32[64,2,2]{1,2,0:T(2,128)}), f32[64,2,2]{1,2,0:T(2,128)S(1)}, u32[]{:S(2)}, u32[]{:S(2)}) async-start(f32[64,2,2]{1,2,0:T(2,128)} %copy.111), calls=%async_computation.6 | async-start | bytes 131072 | tf_op jit(solution)/shard_map/all_to_all | solution.py:61
  200.6 1.5 pad_maximum_fusion
  202.0 6.1 %copy.98 = bf16[2,256,2048]{1,0,2:T(2,128)(2,1)} copy(bf16[2,256,2048]{2,1,0:T(8,128)(2,1)} %pad_maximum_fusion) | data formatting | bytes 4194304 | tf_op jit(solution)/shard_map/concatenate | solution.py:35
  208.2 3.8 %all-to-all-done.6 = f32[64,2,2]{1,2,0:T(2,128)S(1)} async-done(((f32[64,2,2]{1,2,0:T(2,128)}), f32[64,2,2]{1,2,0:T(2,128)S(1)}, u32[]{:S(2)}, u32[]{:S(2)}) %all-to-all-start.6) | async-done | bytes 1056 | tf_op jit(solution)/shard_map/all_to_all | solution.py:61
  211.9 6.6 %all-to-all-start.3 = ((bf16[2,256,2048]{1,0,2:T(2,128)(2,1)}), bf16[2,256,2048]{1,0,2:T(2,128)(2,1)S(1)}, u32[]{:S(2)}, u32[]{:S(2)}) async-start(bf16[2,256,2048]{1,0,2:T(2,128)(2,1)} %copy.98), calls=%async_computation.3 | async-start | bytes 4194304 | tf_op jit(solution)/shard_map/all_to_all | solution.py:38
  218.6 1.3 split.48
  219.9 0.6 fusion.17
  220.5 1.8 copy.110
  222.3 45.9 %all-to-all-done.3 = bf16[2,256,2048]{1,0,2:T(2,128)(2,1)S(1)} async-done(((bf16[2,256,2048]{1,0,2:T(2,128)(2,1)}), bf16[2,256,2048]{1,0,2:T(2,128)(2,1)S(1)}, u32[]{:S(2)}, u32[]{:S(2)}) %all-to-all-start.3) | async-done | bytes 2097184 | tf_op jit(solution)/shard_map/all_to_all | solution.py:38
  268.2 9.1 %all-to-all-start.5 = ((f32[64,2,2048]{2,1,0:T(2,128)}), f32[64,2,2048]{2,1,0:T(2,128)}, u32[]{:S(2)}, u32[]{:S(2)}) async-start(f32[64,2,2048]{2,1,0:T(2,128)} %copy.110), calls=%async_computation.5 | async-start | bytes 2097152 | tf_op jit(solution)/shard_map/all_to_all | solution.py:61
  277.3 11.5 %all_gather.7 = bf16[3,1024,128]{1,2,0:T(8,128)(2,1)S(1)} all-gather(bf16[3,256,128]{1,2,0:T(8,128)(2,1)S(1)} %pad_maximum_fusion.2), channel_id=1, replica_groups=mesh['fsdp'=64,'expert'=4,'dp'=4] {'dp'}, dimensions={1}, use_global_device_ids=true | all-gather | bytes 983040 | tf_op jit(solution)/shard_map/all_gather | solution.py:51
  288.9 0.8 copy.120
  290.1 0.7 copy.114
  291.1 0.7 copy-done.3
  292.4 0.4 fusion.2
  292.9 0.7 reduce_sum.79
  293.6 0.7 reduce_sum.81
  294.3 1.7 fusion.3
  296.1 0.7 reduce_sum.83
  296.8 9.4 %all-to-all-done.5 = f32[64,2,2048]{2,1,0:T(2,128)} async-done(((f32[64,2,2048]{2,1,0:T(2,128)}), f32[64,2,2048]{2,1,0:T(2,128)}, u32[]{:S(2)}, u32[]{:S(2)}) %all-to-all-start.5) | async-done | bytes 1048608 | tf_op jit(solution)/shard_map/all_to_all | solution.py:61
  306.2 2.1 reduce_sum.86
  (44 shorter events, 4.9 us)
Async XLA Ops:
  7.2 151.3 %copy-start = (bf16[1,2048,128]{2,1,0:T(8,128)(2,1)S(1)}, bf16[1,2048,128]{2,1,0:T(8,128)(2,1)}, u32[]{:S(2)}) copy-start(bf16[1,2048,128]{2,1,0:T(8,128)(2,1)} %param.14) | copy-start | bytes 1572868
  8.7 33.6 %all-to-all-start.1 = ((bf16[2,64,32]{2,0,1:T(2,128)(2,1)}), bf16[2,64,32]{2,0,1:T(2,128)(2,1)S(1)}, u32[]{:S(2)}, u32[]{:S(2)}) async-start(bf16[2,64,32]{2,0,1:T(2,128)(2,1)} %copy.90), calls=%async_computation.1 | async-start | bytes 65536 | tf_op jit(solution)/shard_map/all_to_all | solution.py:110
  42.3 16.6 %all-to-all-start = ((bf16[2,64,32]{2,0,1:T(2,128)(2,1)}), bf16[2,64,32]{2,0,1:T(2,128)(2,1)S(1)}, u32[]{:S(2)}, u32[]{:S(2)}) async-start(bf16[2,64,32]{2,0,1:T(2,128)(2,1)} %copy.89), calls=%async_computation | async-start | bytes 65536 | tf_op jit(solution)/shard_map/all_to_all | solution.py:109
  48.0 103.6 %all-gather.2.cloned.1.call-start = ((), (), s32[]{:S(2)}) async-start(), calls=%async_computation.7 | async-start | bytes 2129920 | tf_op jit(solution)/shard_map/all_gather | solution.py:22
  154.9 3.1 copy-start.2
  161.3 28.2 %all-to-all-start.4 = ((bf16[1,4,64,2049]{3,2,0,1:T(8,128)(2,1)}), bf16[1,4,64,2049]{3,2,0,1:T(8,128)(2,1)}, u32[]{:S(2)}, u32[]{:S(2)}) async-start(bf16[1,4,64,2049]{3,2,0,1:T(8,128)(2,1)} %pad_maximum_fusion.1), calls=%async_computation.4 | async-start | bytes 2228224 | tf_op jit(solution)/shard_map/all_to_all | solution.py:14
  191.8 20.1 %all-to-all-start.6 = ((f32[64,2,2]{1,2,0:T(2,128)}), f32[64,2,2]{1,2,0:T(2,128)S(1)}, u32[]{:S(2)}, u32[]{:S(2)}) async-start(f32[64,2,2]{1,2,0:T(2,128)} %copy.111), calls=%async_computation.6 | async-start | bytes 131072 | tf_op jit(solution)/shard_map/all_to_all | solution.py:61
  211.9 56.2 %all-to-all-start.3 = ((bf16[2,256,2048]{1,0,2:T(2,128)(2,1)}), bf16[2,256,2048]{1,0,2:T(2,128)(2,1)S(1)}, u32[]{:S(2)}, u32[]{:S(2)}) async-start(bf16[2,256,2048]{1,0,2:T(2,128)(2,1)} %copy.98), calls=%async_computation.3 | async-start | bytes 4194304 | tf_op jit(solution)/shard_map/all_to_all | solution.py:38
  268.2 38.0 %all-to-all-start.5 = ((f32[64,2,2048]{2,1,0:T(2,128)}), f32[64,2,2048]{2,1,0:T(2,128)}, u32[]{:S(2)}, u32[]{:S(2)}) async-start(f32[64,2,2048]{2,1,0:T(2,128)} %copy.110), calls=%async_computation.5 | async-start | bytes 2097152 | tf_op jit(solution)/shard_map/all_to_all | solution.py:61
  290.8 0.9 copy-start.3
  291.1 1.4 copy-start.1
Sparse Core Ops, SparseCore 0:
  71.2 80.3 all-gather.1
where the time goes:
time: 316 us; the launch traced here: 315 us
  waiting for transfers between devices  179 us (57%)
  starting transfers between devices  57.6 us (18%)
  local copies, waits for them, and re-layouts  23.9 us (8%)
  blocking collectives  22.2 us (7%)
  between operations  14.3 us (5%)
  other arithmetic  10.2 us (3%)
  matrix products  7.51 us (2%)
    all_gather x1, waiting for transfers between devices, rows_first(): out, at, outs = (lax.all_gather(both, axis, axis=0, tiled=True), 0, [])  80.2 us
    all_to_all x1, waiting for transfers between devices, side_by_side(): lax.all_to_all(both, axis, split_axis=split_dim, concat_axis=concat_dim,...  45.9 us
    all_to_all x1, starting transfers between devices, shards(): lax.all_to_all(own_dy, 'fsdp', split_axis=1, concat_axis=0, tiled=True)  22.7 us
    all_to_all x1, waiting for transfers between devices, in_one_piece(): lax.all_to_all(both, axis, split_axis=split_dim, concat_axis=concat_dim,...  22.6 us
    all_to_all x2, starting transfers between devices, sum_at_owner(): tiles = lax.all_to_all(in_blocks(value, dim, peers), axis, 0, 0, tiled=True)  17.9 us
    all_to_all x2, waiting for transfers between devices, sum_at_owner(): tiles = lax.all_to_all(in_blocks(value, dim, peers), axis, 0, 0, tiled=True)  13.1 us
    all_gather x1, blocking collectives, sent_together(): lax.all_gather(both, axis, axis=dim, tiled=True)  11.5 us
    all_to_all x1, blocking collectives, in_one_piece(): lax.all_to_all(both, axis, split_axis=split_dim, concat_axis=concat_dim,...  10.8 us
  transfers between devices with their start and end apart: 7, of which 7 were waited for; matrix products, arithmetic and copies ran while one was open for 7% of the time, Pallas kernels for 0%

commit v1 on v0

v1 whole, which is shorter than its diff:
```python
import jax
import jax.numpy as jnp
from jax import lax
from jax.sharding import PartitionSpec as P

BF = jnp.bfloat16
F32 = jnp.float32


def dot(a, b, ca, cb):
    return lax.dot_general(a, b, (((ca,), (cb,)), ((), ())), preferred_element_type=F32)


def shards(
    tokens, cotangent, expert_ids, slot_ids, route_probs, gate_weight, up_weight, down_weight
):
    peers = lax.axis_size("fsdp")
    experts = lax.axis_size("expert")
    me = lax.axis_index("fsdp")
    mine = lax.axis_index("expert")
    owned, _, width = tokens.shape
    feats = width // peers
    capacity = 2 * expert_ids.shape[0] // experts
    rows = experts * capacity
    hidden_units = gate_weight.shape[2]
    gate_w, up_w, down_w = gate_weight[0], up_weight[0], down_weight[0]

    own_ids = lax.dynamic_slice_in_dim(expert_ids[:, 0, :], me * owned, owned, 0)
    own_slots = lax.dynamic_slice_in_dim(slot_ids[:, 0, :], me * owned, owned, 0)
    own_probs = lax.dynamic_slice_in_dim(route_probs[:, 0, :], me * owned, owned, 0)
    cut_x = tokens[:, 0, :].reshape(owned, peers, feats)
    cut_y = cotangent[:, 0, :].reshape(owned, peers, feats)
    cut = jnp.concatenate([cut_x, cut_y], axis=2).transpose(1, 0, 2)
    cut = cut.reshape(peers, 1, owned * 2 * feats)
    routing = jnp.concatenate([own_ids.astype(BF), own_slots.astype(BF), own_probs], axis=1)
    routing = jnp.pad(routing.reshape(1, 1, owned * 6), ((0, 0), (0, 0), (0, 2 * owned * feats - 6 * owned)))
    routing = jnp.broadcast_to(routing, cut.shape)
    block = jnp.concatenate([cut, routing], axis=1)
    block = jnp.broadcast_to(block[:, None], (peers, experts, 2, 2 * owned * feats))
    block = block.reshape(peers * experts, 2, 2 * owned * feats)
    got = lax.all_to_all(block, ("fsdp", "expert"), 0, 0, tiled=True)
    got_cut, got_route = got[:, 0, :], got[:, 1, : 6 * owned].astype(F32)

    source = lax.broadcasted_iota(jnp.int32, (peers * experts, 1), 0) % experts * capacity
    row_iota = lax.broadcasted_iota(jnp.int32, (peers * experts, rows), 1)
    picks, prob_row, cut_t = [], 0.0, 0.0
    for j in range(owned):
        route = got_route[:, 6 * j : 6 * j + 6]
        first = jnp.logical_and(route[:, 0:1] == mine.astype(F32), route[:, 2:3] >= 0)
        second = jnp.logical_and(route[:, 1:2] == mine.astype(F32), route[:, 3:4] >= 0)
        slot = jnp.where(first, route[:, 2:3], route[:, 3:4]).astype(jnp.int32)
        target = jnp.where(jnp.logical_or(first, second), source + slot, -1)
        pick = row_iota == target
        prob = jnp.where(first, route[:, 4:5], route[:, 5:6])
        prob_row = prob_row + jnp.sum(jnp.where(pick, prob, 0.0), axis=0, keepdims=True)
        picks.append(pick.astype(BF))
        cut_t = cut_t + dot(got_cut[:, 2 * feats * j : 2 * feats * (j + 1)], picks[j], 0, 0)
    cut_t = jnp.broadcast_to(cut_t.astype(BF)[None], (peers, 2 * feats, rows))
    full = lax.all_to_all(cut_t, "fsdp", 0, 0, tiled=True)
    x_t = full[:, :feats].reshape(width, rows)
    y_t = full[:, feats:].reshape(width, rows)

    gate = dot(gate_w, x_t, 0, 0)
    up = dot(up_w, x_t, 0, 0)
    back = dot(down_w, y_t, 1, 0)
    sig = jax.nn.sigmoid(gate)
    swish = gate * sig
    hidden = swish * up
    scaled = (prob_row * hidden).astype(BF)
    score = jnp.sum(hidden.astype(BF).astype(F32) * back, axis=0, keepdims=True)
    scaled_back = prob_row * back
    grad_pre = (scaled_back * up * sig * (1.0 + gate * (1.0 - sig))).astype(BF)
    grad_upper = (scaled_back * swish).astype(BF)

    dx = (dot(gate_w, grad_pre, 1, 0) + dot(up_w, grad_upper, 1, 0)).astype(BF)
    dx, grad_pre, grad_upper, scaled = lax.optimization_barrier((dx, grad_pre, grad_upper, scaled))
    parts = lax.all_to_all(dx.reshape(peers, feats, rows), "fsdp", 0, 0, tiled=True)

    quarter = width // 4
    g_gate = dot(x_t, grad_pre, 1, 1).astype(BF).reshape(2, 2, quarter, hidden_units)
    g_up = dot(x_t, grad_upper, 1, 1).astype(BF).reshape(2, 2, quarter, hidden_units)
    g_down = dot(y_t, scaled, 1, 1).astype(BF).reshape(2, 2, quarter, hidden_units)
    partial = jnp.concatenate([g_gate, g_up, g_down], axis=2)
    dp = lax.axis_index("dp")
    core, half = dp % 2, dp // 2
    away = lax.dynamic_index_in_dim(partial, 1 - core, 1, keepdims=False)
    kept = lax.dynamic_index_in_dim(partial, core, 1, keepdims=False)
    near = lax.ppermute(away, "dp", [(0, 1), (1, 0), (2, 3), (3, 2)])
    both = kept.astype(F32) + near.astype(F32)
    away = lax.dynamic_index_in_dim(both, 1 - half, 0, keepdims=False).astype(BF)
    kept = lax.dynamic_index_in_dim(both, half, 0, keepdims=False)
    far = lax.ppermute(away, "dp", [(0, 2), (2, 0), (1, 3), (3, 1)])
    total = (kept + far.astype(F32)).astype(BF)
    grad_gate = total[:quarter][None]
    grad_up = total[quarter : 2 * quarter][None]
    grad_down = total[2 * quarter :].T[None]

    own_dx = jnp.sum(parts.astype(F32), axis=0).astype(BF)
    high = score.astype(BF)
    low = (score - high.astype(F32)).astype(BF)
    blank = jnp.zeros((owned * feats, rows), BF)
    returned = 0.0
    for j in range(owned):
        lead = blank[: j * feats]
        middle = blank[: (owned - 1 - j) * feats + 2 * j]
        end = blank[: owned * feats - 2 - 2 * j]
        laid = jnp.concatenate([lead, own_dx, middle, high, low, end], axis=0)
        returned = returned + dot(picks[j], laid, 1, 1)
    home = lax.all_to_all(returned.astype(BF), ("fsdp", "expert"), 0, 0, tiled=True)
    home = home.astype(F32).reshape(peers, experts, 2 * owned * feats)
    token_grad = jnp.sum(home[:, :, : owned * feats], axis=1).astype(BF)
    token_grad = token_grad.reshape(peers, owned, feats).transpose(1, 0, 2).reshape(owned, 1, width)
    scores = jnp.sum(home[:, :, owned * feats : owned * feats + 2 * owned], axis=0)
    scores = scores.reshape(experts, owned, 2).sum(axis=2)
    expert_iota = lax.broadcasted_iota(jnp.int32, (experts, owned, 2), 0)
    chosen = jnp.logical_and(expert_iota == own_ids[None], own_slots[None] >= 0)
    prob_grad = jnp.sum(jnp.where(chosen, scores[:, :, None], 0.0), axis=0)
    return grad_gate, grad_up, grad_down, token_grad, prob_grad[:, None, :]


def solution(mesh):
    return jax.shard_map(
        shards,
        mesh=mesh,
        in_specs=(
            P("fsdp", ("expert", "dp"), None),
            P("fsdp", ("expert", "dp"), None),
            P(None, ("expert", "dp"), None),
            P(None, ("expert", "dp"), None),
            P(None, ("expert", "dp"), None),
            P("expert", None, "fsdp"),
            P("expert", None, "fsdp"),
            P("expert", "fsdp", None),
        ),
        out_specs=(
            P("expert", "dp", "fsdp"),
            P("expert", "dp", "fsdp"),
            P("expert", "fsdp", "dp"),
            P("fsdp", ("expert", "dp"), None),
            P("fsdp", ("expert", "dp"), None),
        ),
        check_vma=False,
    )
```

time: 316 us -> 186 us (0.59)
  waiting for transfers between devices: 179 us -> 97.7 us
  blocking collectives: 22.2 us -> 0 us
  between operations: 14.3 us -> 1.02 us
  local copies, waits for them, and re-layouts: 23.9 us -> 13 us
  starting transfers between devices: 57.6 us -> 62.8 us
  other arithmetic: 10.2 us -> 6.21 us
  matrix products: 7.51 us -> 4.23 us
    all_gather x1 -> x0, waiting for transfers between devices: 80.2 us -> none  [rows_first(): out, at, outs = (lax.all_gather(both, axis, axis=0, tiled=True), 0, [])]
    all_to_all x6 -> x4, waiting for transfers between devices: 99.2 us -> 78.3 us  [the longest x1 50.8 us: shards(): full = lax.all_to_all(cut_t, 'fsdp', 0, 0, tiled=True)]
    ppermute x0 -> x2, waiting for transfers between devices: none -> 19.4 us  [the longest x1 19.4 us: shards(): far = lax.ppermute(away, 'dp', [(0, 2), (2, 0), (1, 3), (3, 1)])]
    all_gather x1 -> x0, blocking collectives: 11.5 us -> none  [sent_together(): lax.all_gather(both, axis, axis=dim, tiled=True)]
    all_to_all x1 -> x0, blocking collectives: 10.8 us -> none  [in_one_piece(): lax.all_to_all(both, axis, split_axis=split_dim, concat_axis=concat_dim,...]
    ppermute x0 -> x2, starting transfers between devices: none -> 7.56 us  [the longest x1 5.66 us: shards(): far = lax.ppermute(away, 'dp', [(0, 2), (2, 0), (1, 3), (3, 1)])]
    concatenate x1 -> x3, local copies, waits for them, and re-layouts: 6.13 us -> 0.51 us  [the longest x2 0.48 us: shards(): laid = jnp.concatenate([lead, own_dx, middle, high, low, end], axis=0)]
    reduce_sum x6 -> x5, other arithmetic: 4.59 us -> 0.7 us  [the longest x2 0.3 us: shards(): jnp.sum(jnp.where(pick, prob, 0.0), axis=0, keepdims=True)]
  transfers between devices with their start and end apart: 7 -> 6, of which waited for: 7 -> 5; matrix products, arithmetic and copies ran while one was open for 7% -> 3% of each run, Pallas kernels for 0% -> 0%
where the time goes in v1:
time: 186 us; the launch traced here: 185 us
  waiting for transfers between devices  97.7 us (53%)
  starting transfers between devices  62.8 us (34%)
  local copies, waits for them, and re-layouts  13 us (7%)
  other arithmetic  6.21 us (3%)
  matrix products  4.23 us (2%)
    all_to_all x1, waiting for transfers between devices, shards(): full = lax.all_to_all(cut_t, 'fsdp', 0, 0, tiled=True)  50.8 us
    all_to_all x1, starting transfers between devices, shards(): got = lax.all_to_all(block, ('fsdp', 'expert'), 0, 0, tiled=True)  28.4 us
    ppermute x1, waiting for transfers between devices, shards(): far = lax.ppermute(away, 'dp', [(0, 2), (2, 0), (1, 3), (3, 1)])  19.4 us
    all_to_all x1, starting transfers between devices, shards(): lax.all_to_all(returned.astype(BF), ('fsdp', 'expert'), 0, 0, tiled=True)  14.1 us
    all_to_all x1, waiting for transfers between devices, shards(): got = lax.all_to_all(block, ('fsdp', 'expert'), 0, 0, tiled=True)  14 us
    all_to_all x1, waiting for transfers between devices, shards(): lax.all_to_all(returned.astype(BF), ('fsdp', 'expert'), 0, 0, tiled=True)  12.5 us
    all_to_all x1, starting transfers between devices, shards(): lax.all_to_all(dx.reshape(peers, feats, rows), 'fsdp', 0, 0, tiled=True)  7.22 us
    ppermute x1, starting transfers between devices, shards(): far = lax.ppermute(away, 'dp', [(0, 2), (2, 0), (1, 3), (3, 1)])  5.66 us
  transfers between devices with their start and end apart: 6, of which 5 were waited for; matrix products, arithmetic and copies ran while one was open for 3% of the time, Pallas kernels for 0%

profile of v1, /device:TPU:2, one launch (start us, length us, event | category | flops | bytes accessed | tf_op | source)
XLA Modules:
  0.0 184.9 jit_solution(17120291325636042509)
XLA Ops:
  0.7 0.8 constant_dynamic-slice_fusion.2
  1.7 0.7 constant_dynamic-slice_fusion
  2.7 0.8 reshape_squeeze.6
  3.5 0.8 reshape_squeeze.7
  4.6 0.7 broadcast_in_dim.78
  5.3 28.4 %all-to-all-start = ((bf16[256,2,128]{2,1,0:T(2,128)(2,1)}), bf16[256,2,128]{2,1,0:T(2,128)(2,1)S(1)}, u32[]{:S(2)}, u32[]{:S(2)}) async-start(bf16[256,2,128]{2,1,0:T(2,128)(2,1)} %bitcast.5), calls=%async_computation | async-start | bytes 262144 | tf_op jit(solution)/shard_map/all_to_all | solution.py:41
  33.7 14.0 %all-to-all-done = bf16[256,2,128]{2,1,0:T(2,128)(2,1)S(1)} async-done(((bf16[256,2,128]{2,1,0:T(2,128)(2,1)}), bf16[256,2,128]{2,1,0:T(2,128)(2,1)S(1)}, u32[]{:S(2)}, u32[]{:S(2)}) %all-to-all-start) | async-done | bytes 131104 | tf_op jit(solution)/shard_map/all_to_all | solution.py:41
  47.8 0.4 fusion.18
  48.3 0.4 select_reduce_fusion.2
  48.7 0.2 fusion.16
  48.9 0.3 fusion.5
  49.2 1.6 broadcast_in_dim.80
  50.8 5.5 %all-to-all-start.1 = ((bf16[64,64,256]{2,1,0:T(8,128)(2,1)}), bf16[64,64,256]{2,1,0:T(8,128)(2,1)S(1)}, u32[]{:S(2)}, u32[]{:S(2)}) async-start(bf16[64,64,256]{2,1,0:T(8,128)(2,1)} %broadcast_in_dim.80), calls=%async_computation.1 | async-start | bytes 4194304 | tf_op jit(solution)/shard_map/all_to_all | solution.py:59
  56.3 0.1 select_reduce_fusion
  56.5 0.1 select_reduce_fusion.1
  56.7 50.8 %all-to-all-done.1 = bf16[64,64,256]{2,1,0:T(8,128)(2,1)S(1)} async-done(((bf16[64,64,256]{2,1,0:T(8,128)(2,1)}), bf16[64,64,256]{2,1,0:T(8,128)(2,1)S(1)}, u32[]{:S(2)}, u32[]{:S(2)}) %all-to-all-start.1) | async-done | bytes 2097184 | tf_op jit(solution)/shard_map/all_to_all | solution.py:59
  107.5 0.2 fusion.40
  107.7 0.4 convolution_bitcast_fusion.1
  108.1 0.4 convolution_bitcast_fusion.2
  108.4 0.3 copy-done.4
  108.7 0.3 multiply_reduce_fusion
  109.1 0.5 fusion.8
  109.5 0.5 fusion.2
  110.0 0.4 convolution_convert_fusion.2
  110.4 0.4 convolution_convert_fusion.1
  110.8 0.4 convolution_convert_fusion
  111.4 0.9 dynamic-slice_bitcast_fusion
  112.3 1.9 %collective-permute-start = (bf16[2,1536,128]{2,1,0:T(8,128)(2,1)}, bf16[2,1536,128]{2,1,0:T(8,128)(2,1)}, u32[]{:S(2)}, u32[]{:S(2)}) collective-permute-start(bf16[2,1536,128]{2,1,0:T(8,128)(2,1)} %dynamic-slice_bitcast_fusion), channel_id=1, source_target_pairs={{0,1},{1,0},{2,3},{3,2},{4,5},{5,4},{6,7},{7,6},{8,9},{9,8},{10,11... | collective-permute-start | bytes 2359304 | tf_op jit(solution)/shard_map/ppermute | solution.py:88
  114.2 1.3 copy.60
  115.6 7.2 %all-to-all-start.2 = ((bf16[64,32,256]{2,1,0:T(8,128)(2,1)}), bf16[64,32,256]{2,1,0:T(8,128)(2,1)S(1)}, u32[]{:S(2)}, u32[]{:S(2)}) async-start(bf16[64,32,256]{2,1,0:T(8,128)(2,1)} %bitcast.102), calls=%async_computation.2 | async-start | bytes 2097152 | tf_op jit(solution)/shard_map/all_to_all | solution.py:77
  122.8 1.3 convert_add_fusion
  124.1 1.1 copy-done.1
  125.3 5.7 %collective-permute-start.1 = (bf16[1536,128]{1,0:T(8,128)(2,1)S(1)}, bf16[1536,128]{1,0:T(8,128)(2,1)S(1)}, u32[]{:S(2)}, u32[]{:S(2)}) collective-permute-start(bf16[1536,128]{1,0:T(8,128)(2,1)S(1)} %fusion.14), channel_id=1, source_target_pairs={{0,2},{2,0},{1,3},{3,1},{4,6},{6,4},{5,7},{7,5},{8,10},{10,8},{9,1... | collective-permute-start | bytes 1179656 | tf_op jit(solution)/shard_map/ppermute | solution.py:92
  131.2 19.4 %collective-permute-done.1 = bf16[1536,128]{1,0:T(8,128)(2,1)S(1)} collective-permute-done((bf16[1536,128]{1,0:T(8,128)(2,1)S(1)}, bf16[1536,128]{1,0:T(8,128)(2,1)S(1)}, u32[]{:S(2)}, u32[]{:S(2)}) %collective-permute-start.1) | collective-permute-done | bytes 393248 | tf_op jit(solution)/shard_map/ppermute | solution.py:92
  150.6 1.2 fusion.7
  151.8 0.9 all-to-all-done.2
  152.7 0.2 reduce_sum.79
  152.9 0.2 concatenate.22
  153.2 0.2 fusion.15
  153.4 0.2 concatenate.23
  153.7 0.2 fusion.4
  153.9 0.7 copy.61
  154.6 14.1 %all-to-all-start.3 = ((bf16[256,1,128]{2,1,0:T(2,128)(2,1)}), bf16[256,1,128]{2,1,0:T(2,128)(2,1)S(1)}, u32[]{:S(2)}, u32[]{:S(2)}) async-start(bf16[256,1,128]{2,1,0:T(2,128)(2,1)} %copy.61), calls=%async_computation.3 | async-start | bytes 262144 | tf_op jit(solution)/shard_map/all_to_all | solution.py:109
  168.7 0.7 slice_bitcast_fusion
  169.5 0.8 copy.66
  170.2 12.5 %all-to-all-done.3 = bf16[256,1,128]{2,1,0:T(2,128)(2,1)S(1)} async-done(((bf16[256,1,128]{2,1,0:T(2,128)(2,1)}), bf16[256,1,128]{2,1,0:T(2,128)(2,1)S(1)}, u32[]{:S(2)}, u32[]{:S(2)}) %all-to-all-start.3) | async-done | bytes 65568 | tf_op jit(solution)/shard_map/all_to_all | solution.py:109
  183.3 0.7 reshape.149
  184.1 0.7 fusion.41
  (41 shorter events, 2.0 us)
Async XLA Ops:
  0.6 107.0 %copy-start = (bf16[1,2048,128]{2,1,0:T(8,128)(2,1)S(1)}, bf16[1,2048,128]{2,1,0:T(8,128)(2,1)}, u32[]{:S(2)}) copy-start(bf16[1,2048,128]{2,1,0:T(8,128)(2,1)} %param.13) | copy-start | bytes 1572868
  5.3 42.4 %all-to-all-start = ((bf16[256,2,128]{2,1,0:T(2,128)(2,1)}), bf16[256,2,128]{2,1,0:T(2,128)(2,1)S(1)}, u32[]{:S(2)}, u32[]{:S(2)}) async-start(bf16[256,2,128]{2,1,0:T(2,128)(2,1)} %bitcast.5), calls=%async_computation | async-start | bytes 262144 | tf_op jit(solution)/shard_map/all_to_all | solution.py:41
  50.8 56.7 %all-to-all-start.1 = ((bf16[64,64,256]{2,1,0:T(8,128)(2,1)}), bf16[64,64,256]{2,1,0:T(8,128)(2,1)S(1)}, u32[]{:S(2)}, u32[]{:S(2)}) async-start(bf16[64,64,256]{2,1,0:T(8,128)(2,1)} %broadcast_in_dim.80), calls=%async_computation.1 | async-start | bytes 4194304 | tf_op jit(solution)/shard_map/all_to_all | solution.py:59
  56.7 51.4 %copy-start.2 = (bf16[1,2048,128]{2,1,0:T(8,128)(2,1)S(1)}, bf16[1,2048,128]{2,1,0:T(8,128)(2,1)}, u32[]{:S(2)}) copy-start(bf16[1,2048,128]{2,1,0:T(8,128)(2,1)} %param.14) | copy-start | bytes 1572868
  107.7 1.0 copy-start.4
  112.3 10.5 %collective-permute-start = (bf16[2,1536,128]{2,1,0:T(8,128)(2,1)}, bf16[2,1536,128]{2,1,0:T(8,128)(2,1)}, u32[]{:S(2)}, u32[]{:S(2)}) collective-permute-start(bf16[2,1536,128]{2,1,0:T(8,128)(2,1)} %dynamic-slice_bitcast_fusion), channel_id=1, source_target_pairs={{0,1},{1,0},{2,3},{3,2},{4,5},{5,4},{6,7},{7,6},{8,9},{9,8},{10,11... | collective-permute-start | bytes 2359304 | tf_op jit(solution)/shard_map/ppermute | solution.py:88
  115.6 37.2 %all-to-all-start.2 = ((bf16[64,32,256]{2,1,0:T(8,128)(2,1)}), bf16[64,32,256]{2,1,0:T(8,128)(2,1)S(1)}, u32[]{:S(2)}, u32[]{:S(2)}) async-start(bf16[64,32,256]{2,1,0:T(8,128)(2,1)} %bitcast.102), calls=%async_computation.2 | async-start | bytes 2097152 | tf_op jit(solution)/shard_map/all_to_all | solution.py:77
  122.8 8.2 %copy-start.3 = (s32[128,1,2]{0,2,1:T(2,128)S(1)}, s32[128,1,2]{0,2,1:T(2,128)}, u32[]{:S(2)}) copy-start(s32[128,1,2]{0,2,1:T(2,128)} %param.11) | copy-start | bytes 3076
  124.1 1.2 copy-start.1
  125.3 25.3 %collective-permute-start.1 = (bf16[1536,128]{1,0:T(8,128)(2,1)S(1)}, bf16[1536,128]{1,0:T(8,128)(2,1)S(1)}, u32[]{:S(2)}, u32[]{:S(2)}) collective-permute-start(bf16[1536,128]{1,0:T(8,128)(2,1)S(1)} %fusion.14), channel_id=1, source_target_pairs={{0,2},{2,0},{1,3},{3,1},{4,6},{6,4},{5,7},{7,5},{8,10},{10,8},{9,1... | collective-permute-start | bytes 1179656 | tf_op jit(solution)/shard_map/ppermute | solution.py:92
  154.6 28.1 %all-to-all-start.3 = ((bf16[256,1,128]{2,1,0:T(2,128)(2,1)}), bf16[256,1,128]{2,1,0:T(2,128)(2,1)S(1)}, u32[]{:S(2)}, u32[]{:S(2)}) async-start(bf16[256,1,128]{2,1,0:T(2,128)(2,1)} %copy.61), calls=%async_computation.3 | async-start | bytes 262144 | tf_op jit(solution)/shard_map/all_to_all | solution.py:109

commit v2 on v1

--- a/solution.py
+++ b/solution.py
@@ -16,7 +16,6 @@
 ):
     peers = lax.axis_size("fsdp")
     experts = lax.axis_size("expert")
-    me = lax.axis_index("fsdp")
     mine = lax.axis_index("expert")
     owned, _, width = tokens.shape
     feats = width // peers
@@ -25,27 +24,38 @@
     hidden_units = gate_weight.shape[2]
     gate_w, up_w, down_w = gate_weight[0], up_weight[0], down_weight[0]
 
-    own_ids = lax.dynamic_slice_in_dim(expert_ids[:, 0, :], me * owned, owned, 0)
-    own_slots = lax.dynamic_slice_in_dim(slot_ids[:, 0, :], me * owned, owned, 0)
-    own_probs = lax.dynamic_slice_in_dim(route_probs[:, 0, :], me * owned, owned, 0)
-    cut_x = tokens[:, 0, :].reshape(owned, peers, feats)
-    cut_y = cotangent[:, 0, :].reshape(owned, peers, feats)
-    cut = jnp.concatenate([cut_x, cut_y], axis=2).transpose(1, 0, 2)
-    cut = cut.reshape(peers, 1, owned * 2 * feats)
-    routing = jnp.concatenate([own_ids.astype(BF), own_slots.astype(BF), own_probs], axis=1)
-    routing = jnp.pad(routing.reshape(1, 1, owned * 6), ((0, 0), (0, 0), (0, 2 * owned * feats - 6 * owned)))
-    routing = jnp.broadcast_to(routing, cut.shape)
-    block = jnp.concatenate([cut, routing], axis=1)
-    block = jnp.broadcast_to(block[:, None], (peers, experts, 2, 2 * owned * feats))
-    block = block.reshape(peers * experts, 2, 2 * owned * feats)
-    got = lax.all_to_all(block, ("fsdp", "expert"), 0, 0, tiled=True)
-    got_cut, got_route = got[:, 0, :], got[:, 1, : 6 * owned].astype(F32)
+    side = 1
+    while side * side < peers:
+        side *= 2
+    xa, ya, xb, yb = feats * 4 * side // 8, feats * 3 * side // 8, feats * 4 * side // 8, feats * 5 * side // 8
+    in_row = [[i * side + j for j in range(side)] for i in range(side)]
+    in_column = [[i * side + j for i in range(side)] for j in range(side)]
 
-    source = lax.broadcasted_iota(jnp.int32, (peers * experts, 1), 0) % experts * capacity
+    fields = [expert_ids[:, 0, :].astype(BF), slot_ids[:, 0, :].astype(BF), route_probs[:, 0, :]]
+    fields = jnp.concatenate(fields, axis=1).reshape(peers, owned * 6)
+    got_route = lax.all_gather(fields, "expert", axis=0, tiled=True).astype(F32)
+
+    own_x, own_y = tokens[:, 0, :], cotangent[:, 0, :]
+    full = (owned, side, side)
+    a_x = own_x[:, : side * xa].reshape(owned, 1, side, xa)
+    a_y = own_y[:, : side * ya].reshape(owned, 1, side, ya)
+    b_y = own_y[:, side * ya :].reshape(owned, side, 1, yb)
+    b_x = own_x[:, side * xa :].reshape(owned, side, 1, xb)
+    cut = [jnp.broadcast_to(v, full + v.shape[3:]) for v in (a_x, a_y, b_y, b_x)]
+    cut = jnp.concatenate(cut, axis=3).transpose(1, 2, 0, 3)
+    part = xa + ya + xb + yb
+    block = cut.reshape(peers, owned * part // 128, 128)
+    block = jnp.broadcast_to(block[None], (experts,) + block.shape)
+    block = block.reshape((experts * peers,) + block.shape[2:])
+    got = lax.all_to_all(block, ("expert", "fsdp"), 0, 0, tiled=True)
+    got_cut = got.reshape(experts * peers, owned, part)
+
+    source = lax.broadcasted_iota(jnp.int32, (peers * experts, 1), 0) // peers * capacity
     row_iota = lax.broadcasted_iota(jnp.int32, (peers * experts, rows), 1)
     picks, prob_row, cut_t = [], 0.0, 0.0
     for j in range(owned):
-        route = got_route[:, 6 * j : 6 * j + 6]
+        first_at = 6 * j
+        route = got_route[:, first_at : first_at + 6]
         first = jnp.logical_and(route[:, 0:1] == mine.astype(F32), route[:, 2:3] >= 0)
         second = jnp.logical_and(route[:, 1:2] == mine.astype(F32), route[:, 3:4] >= 0)
         slot = jnp.where(first, route[:, 2:3], route[:, 3:4]).astype(jnp.int32)
@@ -54,11 +64,18 @@
         prob = jnp.where(first, route[:, 4:5], route[:, 5:6])
         prob_row = prob_row + jnp.sum(jnp.where(pick, prob, 0.0), axis=0, keepdims=True)
         picks.append(pick.astype(BF))
-        cut_t = cut_t + dot(got_cut[:, 2 * feats * j : 2 * feats * (j + 1)], picks[j], 0, 0)
-    cut_t = jnp.broadcast_to(cut_t.astype(BF)[None], (peers, 2 * feats, rows))
-    full = lax.all_to_all(cut_t, "fsdp", 0, 0, tiled=True)
-    x_t = full[:, :feats].reshape(width, rows)
-    y_t = full[:, feats:].reshape(width, rows)
+        cut_t = cut_t + dot(got_cut[:, j], picks[j], 0, 0)
+    cut_t = cut_t.astype(BF)
+    a_cut, b_cut = cut_t[: xa + ya], cut_t[xa + ya :]
+    b_cut = jnp.broadcast_to(b_cut[None], (side,) + b_cut.shape)
+    b_full = lax.all_to_all(b_cut, "fsdp", 0, 0, axis_index_groups=in_column, tiled=True)
+    a_full = lax.all_gather(a_cut, "fsdp", axis=0, axis_index_groups=in_row)
+    x_t = jnp.concatenate(
+        [a_full[:, :xa].reshape(-1, rows), b_full[:, yb:].reshape(-1, rows)], axis=0
+    )
+    y_t = jnp.concatenate(
+        [a_full[:, xa:].reshape(-1, rows), b_full[:, :yb].reshape(-1, rows)], axis=0
+    )
 
     gate = dot(gate_w, x_t, 0, 0)
     up = dot(up_w, x_t, 0, 0)
@@ -90,11 +107,6 @@
     away = lax.dynamic_index_in_dim(both, 1 - half, 0, keepdims=False).astype(BF)
     kept = lax.dynamic_index_in_dim(both, half, 0, keepdims=False)
     far = lax.ppermute(away, "dp", [(0, 2), (2, 0), (1, 3), (3, 1)])
-    total = (kept + far.astype(F32)).astype(BF)
-    grad_gate = total[:quarter][None]
-    grad_up = total[quarter : 2 * quarter][None]
-    grad_down = total[2 * quarter :].T[None]
-
     own_dx = jnp.sum(parts.astype(F32), axis=0).astype(BF)
     high = score.astype(BF)
     low = (score - high.astype(F32)).astype(BF)
@@ -106,12 +118,21 @@
         end = blank[: owned * feats - 2 - 2 * j]
         laid = jnp.concatenate([lead, own_dx, middle, high, low, end], axis=0)
         returned = returned + dot(picks[j], laid, 1, 1)
-    home = lax.all_to_all(returned.astype(BF), ("fsdp", "expert"), 0, 0, tiled=True)
-    home = home.astype(F32).reshape(peers, experts, 2 * owned * feats)
-    token_grad = jnp.sum(home[:, :, : owned * feats], axis=1).astype(BF)
+    returned = returned.astype(BF)
+    far, _ = lax.optimization_barrier((far, returned))
+    total = (kept + far.astype(F32)).astype(BF)
+    grad_gate = total[:quarter][None]
+    grad_up = total[quarter : 2 * quarter][None]
+    grad_down = total[2 * quarter :].T[None]
+    home = lax.all_to_all(returned, ("expert", "fsdp"), 0, 0, tiled=True)
+    home = home.astype(F32).reshape(experts, peers, 2 * owned * feats)
+    token_grad = jnp.sum(home[:, :, : owned * feats], axis=0).astype(BF)
     token_grad = token_grad.reshape(peers, owned, feats).transpose(1, 0, 2).reshape(owned, 1, width)
-    scores = jnp.sum(home[:, :, owned * feats : owned * feats + 2 * owned], axis=0)
+    scores = jnp.sum(home[:, :, owned * feats : owned * feats + 2 * owned], axis=1)
     scores = scores.reshape(experts, owned, 2).sum(axis=2)
+    me = lax.axis_index("fsdp")
+    own_ids = lax.dynamic_slice_in_dim(expert_ids[:, 0, :], me * owned, owned, 0)
+    own_slots = lax.dynamic_slice_in_dim(slot_ids[:, 0, :], me * owned, owned, 0)
     expert_iota = lax.broadcasted_iota(jnp.int32, (experts, owned, 2), 0)
     chosen = jnp.logical_and(expert_iota == own_ids[None], own_slots[None] >= 0)
     prob_grad = jnp.sum(jnp.where(chosen, scores[:, :, None], 0.0), axis=0)

time: 186 us -> 177 us (0.952)
  waiting for transfers between devices: 97.7 us -> 37.7 us
  blocking collectives: 0 us -> 40.8 us
  starting transfers between devices: 62.8 us -> 68.4 us
  local copies, waits for them, and re-layouts: 13 us -> 18.2 us
    all_to_all x3, waiting for transfers between devices: 77.4 us -> 21 us  [the longest x1 12.9 us: shards(): home = lax.all_to_all(returned, ('expert', 'fsdp'), 0, 0, tiled=True)]
    all_gather x0 -> x2, blocking collectives: none -> 40.8 us  [the longest x1 26.4 us: shards(): a_full = lax.all_gather(a_cut, 'fsdp', axis=0, axis_index_groups=in_row)]
    ppermute x1, waiting for transfers between devices: 19.4 us -> 5.32 us  [shards(): far = lax.ppermute(away, 'dp', [(0, 2), (2, 0), (1, 3), (3, 1)])]
    all_to_all x1, waiting for transfers between devices: 0.9 us -> 11.4 us  [shards(): lax.all_to_all(dx.reshape(peers, feats, rows), 'fsdp', 0, 0, tiled=True)]
    all_to_all x1, starting transfers between devices: 7.22 us -> 10.6 us  [shards(): lax.all_to_all(dx.reshape(peers, feats, rows), 'fsdp', 0, 0, tiled=True)]
    all_to_all x3, starting transfers between devices: 48 us -> 50.3 us  [the longest x1 28.4 us: shards(): got = lax.all_to_all(block, ('expert', 'fsdp'), 0, 0, tiled=True)]
    slice x1 -> x8, local copies, waits for them, and re-layouts: 0.17 us -> 2.36 us  [the longest x1 0.79 us: shards(): a_full[:, xa:].reshape(-1, rows)]
  transfers between devices with their start and end apart: 6 -> 6, of which waited for: 5 -> 5; matrix products, arithmetic and copies ran while one was open for 3% -> 8% of each run, Pallas kernels for 0% -> 0%
where the time goes in v2:
time: 177 us; the launch traced here: 176 us
  starting transfers between devices  68.4 us (39%)
  blocking collectives  40.8 us (23%)
  waiting for transfers between devices  37.7 us (21%)
  local copies, waits for them, and re-layouts  18.2 us (10%)
  matrix products  5.65 us (3%)
  other arithmetic  4.4 us (2%)
    all_to_all x1, starting transfers between devices, shards(): got = lax.all_to_all(block, ('expert', 'fsdp'), 0, 0, tiled=True)  28.4 us
    all_gather x1, blocking collectives, shards(): a_full = lax.all_gather(a_cut, 'fsdp', axis=0, axis_index_groups=in_row)  26.4 us
    all_to_all x1, starting transfers between devices, shards(): home = lax.all_to_all(returned, ('expert', 'fsdp'), 0, 0, tiled=True)  18.2 us
    all_gather x1, blocking collectives, shards(): got_route = lax.all_gather(fields, 'expert', axis=0, tiled=True).astype(F32)  14.5 us
    all_to_all x1, waiting for transfers between devices, shards(): home = lax.all_to_all(returned, ('expert', 'fsdp'), 0, 0, tiled=True)  12.9 us
    all_to_all x1, waiting for transfers between devices, shards(): lax.all_to_all(dx.reshape(peers, feats, rows), 'fsdp', 0, 0, tiled=True)  11.4 us
    all_to_all x1, starting transfers between devices, shards(): lax.all_to_all(dx.reshape(peers, feats, rows), 'fsdp', 0, 0, tiled=True)  10.6 us
    all_to_all x1, waiting for transfers between devices, shards(): got = lax.all_to_all(block, ('expert', 'fsdp'), 0, 0, tiled=True)  6.12 us
  transfers between devices with their start and end apart: 6, of which 5 were waited for; matrix products, arithmetic and copies ran while one was open for 8% of the time, Pallas kernels for 0%

profile of v2, /device:TPU:2, one launch (start us, length us, event | category | flops | bytes accessed | tf_op | source)
XLA Modules:
  0.0 176.3 jit_solution(10087988659308721120)
XLA Ops:
  0.7 0.7 slice.148
  1.4 0.7 slice.147
  2.3 0.7 slice_bitcast_fusion.8
  3.5 0.9 broadcast_in_dim.105
  4.3 28.4 %all-to-all-start = ((bf16[256,8,128]{2,1,0:T(8,128)(2,1)}), bf16[256,8,128]{2,1,0:T(8,128)(2,1)S(1)}, u32[]{:S(2)}, u32[]{:S(2)}) async-start(bf16[256,8,128]{2,1,0:T(8,128)(2,1)} %bitcast.5), calls=%async_computation | async-start | bytes 1048576 | tf_op jit(solution)/shard_map/all_to_all | solution.py:50
  33.1 14.5 %all-gather.1 = bf16[4,64,12]{1,2,0:T(8,128)(2,1)S(1)} all-gather(bf16[1,64,12]{1,2,0:T(8,128)(2,1)S(1)} %copy.155), channel_id=1, replica_groups=mesh['fsdp'=64,'expert'=4,'dp'=4] {'expert'}, dimensions={0}, use_global_device_ids=true | all-gather | bytes 7680 | tf_op jit(solution)/shard_map/all_gather | solution.py:36
  47.7 6.1 %all-to-all-done = bf16[256,8,128]{2,1,0:T(8,128)(2,1)S(1)} async-done(((bf16[256,8,128]{2,1,0:T(8,128)(2,1)}), bf16[256,8,128]{2,1,0:T(8,128)(2,1)S(1)}, u32[]{:S(2)}, u32[]{:S(2)}) %all-to-all-start) | async-done | bytes 524320 | tf_op jit(solution)/shard_map/all_to_all | solution.py:50
  53.8 0.3 copy.152
  54.8 1.1 broadcast_in_dim.106
  55.9 3.8 %all-to-all-start.1 = ((bf16[8,288,256]{2,1,0:T(8,128)(2,1)}), bf16[8,288,256]{2,1,0:T(8,128)(2,1)S(1)}, u32[]{:S(2)}, u32[]{:S(2)}) async-start(bf16[8,288,256]{2,1,0:T(8,128)(2,1)} %broadcast_in_dim.106), calls=%async_computation.1 | async-start | bytes 2359296 | tf_op jit(solution)/shard_map/all_to_all | solution.py:71
  60.1 26.4 %all-gather = bf16[1792,256]{1,0:T(8,128)(2,1)S(1)} all-gather(bf16[224,256]{1,0:T(8,128)(2,1)S(1)} %slice.160), channel_id=2, replica_groups={{0,16,32,48,64,80,96,112},{128,144,160,176,192,208,224,240},{256,272,28..., dimensions={0}, use_global_device_ids=true | all-gather | bytes 1032192 | tf_op jit(solution)/shard_map/all_gather | solution.py:72
  86.5 0.8 slice.168
  87.3 2.0 %all-to-all-done.1 = bf16[8,288,256]{2,1,0:T(8,128)(2,1)S(1)} async-done(((bf16[8,288,256]{2,1,0:T(8,128)(2,1)}), bf16[8,288,256]{2,1,0:T(8,128)(2,1)S(1)}, u32[]{:S(2)}, u32[]{:S(2)}) %all-to-all-start.1) | async-done | bytes 1179680 | tf_op jit(solution)/shard_map/all_to_all | solution.py:71
  89.3 0.3 convolution_bitcast_fusion.1
  89.7 0.4 copy-done.4
  90.1 0.3 convolution_bitcast_fusion.2
  90.5 0.6 copy-done.6
  91.3 0.3 multiply_reduce_fusion
  91.6 0.5 fusion.7
  92.1 0.5 fusion.2
  92.6 1.3 copy.161
  93.9 10.6 %all-to-all-start.2 = ((bf16[64,32,256]{2,1,0:T(8,128)(2,1)}), bf16[64,32,256]{2,1,0:T(8,128)(2,1)S(1)}, u32[]{:S(2)}, u32[]{:S(2)}) async-start(bf16[64,32,256]{2,1,0:T(8,128)(2,1)} %bitcast.35), calls=%async_computation.2 | async-start | bytes 2097152 | tf_op jit(solution)/shard_map/all_to_all | solution.py:94
  104.5 0.4 convolution_convert_fusion.2
  104.9 0.4 convolution_convert_fusion.1
  105.5 0.4 convolution_convert_fusion
  106.0 0.9 dynamic-slice_bitcast_fusion
  106.9 1.9 %collective-permute-start = (bf16[2,1536,128]{2,1,0:T(8,128)(2,1)}, bf16[2,1536,128]{2,1,0:T(8,128)(2,1)}, u32[]{:S(2)}, u32[]{:S(2)}) collective-permute-start(bf16[2,1536,128]{2,1,0:T(8,128)(2,1)} %dynamic-slice_bitcast_fusion), channel_id=1, source_target_pairs={{0,1},{1,0},{2,3},{3,2},{4,5},{5,4},{6,7},{7,6},{8,9},{9,8},{10,11... | collective-permute-start | bytes 2359304 | tf_op jit(solution)/shard_map/ppermute | solution.py:105
  109.0 0.6 copy.165
  109.7 0.7 copy.166
  110.4 0.6 convert_element_type.163
  110.9 0.6 subtract_convert_fusion
  111.5 1.3 convert_add_fusion
  112.8 1.1 copy-done.1
  113.9 0.8 fusion.13
  114.8 5.6 %collective-permute-start.1 = (bf16[1536,128]{1,0:T(8,128)(2,1)}, bf16[1536,128]{1,0:T(8,128)(2,1)S(1)}, u32[]{:S(2)}, u32[]{:S(2)}) collective-permute-start(bf16[1536,128]{1,0:T(8,128)(2,1)} %fusion.13), channel_id=1, source_target_pairs={{0,2},{2,0},{1,3},{3,1},{4,6},{6,4},{5,7},{7,5},{8,10},{10,8},{9,1... | collective-permute-start | bytes 1179656 | tf_op jit(solution)/shard_map/ppermute | solution.py:109
  120.3 11.4 %all-to-all-done.2 = bf16[64,32,256]{2,1,0:T(8,128)(2,1)S(1)} async-done(((bf16[64,32,256]{2,1,0:T(8,128)(2,1)}), bf16[64,32,256]{2,1,0:T(8,128)(2,1)S(1)}, u32[]{:S(2)}, u32[]{:S(2)}) %all-to-all-start.2) | async-done | bytes 1048608 | tf_op jit(solution)/shard_map/all_to_all | solution.py:94
  131.9 0.9 concatenate.26
  132.8 0.9 concatenate.27
  133.8 0.9 fusion.15
  134.7 0.9 fusion.4
  135.6 5.3 %collective-permute-done.1 = bf16[1536,128]{1,0:T(8,128)(2,1)S(1)} collective-permute-done((bf16[1536,128]{1,0:T(8,128)(2,1)}, bf16[1536,128]{1,0:T(8,128)(2,1)S(1)}, u32[]{:S(2)}, u32[]{:S(2)}) %collective-permute-start.1) | collective-permute-done | bytes 393248 | tf_op jit(solution)/shard_map/ppermute | solution.py:109
  140.9 0.8 copy.162
  141.7 18.2 %all-to-all-start.3 = ((bf16[256,1,128]{2,1,0:T(2,128)(2,1)}), bf16[256,1,128]{2,1,0:T(2,128)(2,1)S(1)}, u32[]{:S(2)}, u32[]{:S(2)}) async-start(bf16[256,1,128]{2,1,0:T(2,128)(2,1)} %copy.162), calls=%async_computation.3 | async-start | bytes 262144 | tf_op jit(solution)/shard_map/all_to_all | solution.py:127
  160.0 0.7 slice_bitcast_fusion.4
  160.7 0.8 copy.168
  161.5 12.9 %all-to-all-done.3 = bf16[256,1,128]{2,1,0:T(2,128)(2,1)S(1)} async-done(((bf16[256,1,128]{2,1,0:T(2,128)(2,1)}), bf16[256,1,128]{2,1,0:T(2,128)(2,1)S(1)}, u32[]{:S(2)}, u32[]{:S(2)}) %all-to-all-start.3) | async-done | bytes 65568 | tf_op jit(solution)/shard_map/all_to_all | solution.py:127
  174.8 0.7 reshape.191
  175.6 0.7 fusion.25
  (74 shorter events, 3.5 us)
Async XLA Ops:
  0.6 88.7 %copy-start = (bf16[1,2048,128]{2,1,0:T(8,128)(2,1)S(1)}, bf16[1,2048,128]{2,1,0:T(8,128)(2,1)}, u32[]{:S(2)}) copy-start(bf16[1,2048,128]{2,1,0:T(8,128)(2,1)} %param.13) | copy-start | bytes 1572868
  0.6 32.1 %copy-start.10 = (s32[128,1,2]{0,2,1:T(2,128)S(1)}, s32[128,1,2]{0,2,1:T(2,128)}, u32[]{:S(2)}) copy-start(s32[128,1,2]{0,2,1:T(2,128)} %param.10) | copy-start | bytes 3076
  0.7 32.1 %copy-start.11 = (s32[128,1,2]{0,2,1:T(2,128)S(1)}, s32[128,1,2]{0,2,1:T(2,128)}, u32[]{:S(2)}) copy-start(s32[128,1,2]{0,2,1:T(2,128)} %param.11) | copy-start | bytes 3076
  0.7 32.1 %copy-start.13 = (bf16[128,1,2]{0,2,1:T(2,128)(2,1)S(1)}, bf16[128,1,2]{0,2,1:T(2,128)(2,1)}, u32[]{:S(2)}) copy-start(bf16[128,1,2]{0,2,1:T(2,128)(2,1)} %param.12) | copy-start | bytes 1540
  4.3 49.5 %all-to-all-start = ((bf16[256,8,128]{2,1,0:T(8,128)(2,1)}), bf16[256,8,128]{2,1,0:T(8,128)(2,1)S(1)}, u32[]{:S(2)}, u32[]{:S(2)}) async-start(bf16[256,8,128]{2,1,0:T(8,128)(2,1)} %bitcast.5), calls=%async_computation | async-start | bytes 1048576 | tf_op jit(solution)/shard_map/all_to_all | solution.py:50
  47.7 12.0 %copy-start.8 = (s32[256,1]{0,1:T(1,128)}, s32[256,1]{0,1:T(1,128)S(1)}, u32[]{:S(2)}) copy-start(s32[256,1]{0,1:T(1,128)S(1)} %get-tuple-element.59) | copy-start | bytes 3076
  47.7 12.2 %copy-start.9 = (s32[256,1]{0,1:T(1,128)}, s32[256,1]{0,1:T(1,128)S(1)}, u32[]{:S(2)}) copy-start(s32[256,1]{0,1:T(1,128)S(1)} %get-tuple-element.60) | copy-start | bytes 3076
  55.9 33.4 %all-to-all-start.1 = ((bf16[8,288,256]{2,1,0:T(8,128)(2,1)}), bf16[8,288,256]{2,1,0:T(8,128)(2,1)S(1)}, u32[]{:S(2)}, u32[]{:S(2)}) async-start(bf16[8,288,256]{2,1,0:T(8,128)(2,1)} %broadcast_in_dim.106), calls=%async_computation.1 | async-start | bytes 2359296 | tf_op jit(solution)/shard_map/all_to_all | solution.py:71
  86.5 3.7 %copy-start.3 = (bf16[1,2048,128]{2,1,0:T(8,128)(2,1)S(1)}, bf16[1,2048,128]{2,1,0:T(8,128)(2,1)}, u32[]{:S(2)}) copy-start(bf16[1,2048,128]{2,1,0:T(8,128)(2,1)} %param.14) | copy-start | bytes 1572868
  89.3 0.8 copy-start.4
  90.1 1.0 copy-start.6
  90.1 1.2 copy-start.14
  92.6 11.9 %copy-start.5 = (bf16[8,128,256]{2,1,0:T(8,128)(2,1)S(1)}, bf16[8,128,256]{2,1,0:T(8,128)(2,1)}, u32[]{:S(2)}) copy-start(bf16[8,128,256]{2,1,0:T(8,128)(2,1)} %copy-done.4) | copy-start | bytes 1572868
  93.9 37.8 %all-to-all-start.2 = ((bf16[64,32,256]{2,1,0:T(8,128)(2,1)}), bf16[64,32,256]{2,1,0:T(8,128)(2,1)S(1)}, u32[]{:S(2)}, u32[]{:S(2)}) async-start(bf16[64,32,256]{2,1,0:T(8,128)(2,1)} %bitcast.35), calls=%async_computation.2 | async-start | bytes 2097152 | tf_op jit(solution)/shard_map/all_to_all | solution.py:94
  104.5 1.0 copy-start.7
  106.9 4.6 %collective-permute-start = (bf16[2,1536,128]{2,1,0:T(8,128)(2,1)}, bf16[2,1536,128]{2,1,0:T(8,128)(2,1)}, u32[]{:S(2)}, u32[]{:S(2)}) collective-permute-start(bf16[2,1536,128]{2,1,0:T(8,128)(2,1)} %dynamic-slice_bitcast_fusion), channel_id=1, source_target_pairs={{0,1},{1,0},{2,3},{3,2},{4,5},{5,4},{6,7},{7,6},{8,9},{9,8},{10,11... | collective-permute-start | bytes 2359304 | tf_op jit(solution)/shard_map/ppermute | solution.py:105
  112.8 1.1 copy-start.1
  114.8 45.1 %copy-start.2 = (f32[2,1536,128]{2,1,0:T(8,128)S(1)}, f32[2,1536,128]{2,1,0:T(8,128)}, u32[]{:S(2)}) copy-start(f32[2,1536,128]{2,1,0:T(8,128)} %copy-done.1) | copy-start | bytes 4718596
  114.8 26.2 %collective-permute-start.1 = (bf16[1536,128]{1,0:T(8,128)(2,1)}, bf16[1536,128]{1,0:T(8,128)(2,1)S(1)}, u32[]{:S(2)}, u32[]{:S(2)}) collective-permute-start(bf16[1536,128]{1,0:T(8,128)(2,1)} %fusion.13), channel_id=1, source_target_pairs={{0,2},{2,0},{1,3},{3,1},{4,6},{6,4},{5,7},{7,5},{8,10},{10,8},{9,1... | collective-permute-start | bytes 1179656 | tf_op jit(solution)/shard_map/ppermute | solution.py:109
  133.8 41.9 %copy-start.12 = (s32[2,1,2]{2,0,1:T(2,128)S(1)}, s32[2,1,2]{2,0,1:T(2,128)}, u32[]{:S(2)}) copy-start(s32[2,1,2]{2,0,1:T(2,128)} %copy.165) | copy-start | bytes 52
  133.8 41.9 %copy-start.15 = (pred[2,1,2]{2,0,1:T(4,128)(4,1)S(1)}, pred[2,1,2]{2,0,1:T(4,128)(4,1)}, u32[]{:S(2)}) copy-start(pred[2,1,2]{2,0,1:T(4,128)(4,1)} %copy.166) | copy-start | bytes 16
  141.7 32.6 %all-to-all-start.3 = ((bf16[256,1,128]{2,1,0:T(2,128)(2,1)}), bf16[256,1,128]{2,1,0:T(2,128)(2,1)S(1)}, u32[]{:S(2)}, u32[]{:S(2)}) async-start(bf16[256,1,128]{2,1,0:T(2,128)(2,1)} %copy.162), calls=%async_computation.3 | async-start | bytes 262144 | tf_op jit(solution)/shard_map/all_to_all | solution.py:127

commit v3 on v2

v3 whole, which is shorter than its diff:
```python
import functools

import jax
import jax.numpy as jnp
from jax import lax
from jax.experimental import pallas as pl
from jax.experimental.pallas import tpu as pltpu
from jax.sharding import PartitionSpec as P

BF = jnp.bfloat16
F32 = jnp.float32


def dot(a, b, ca, cb):
    return lax.dot_general(a, b, (((ca,), (cb,)), ((), ())), preferred_element_type=F32)


VMEM = pl.BlockSpec(memory_space=pltpu.VMEM)
SMEM = pl.BlockSpec(memory_space=pltpu.SMEM)


def call(kernel, shapes, in_specs, scratch=(), flops=0):
    return pl.pallas_call(
        kernel,
        out_shape=[jax.ShapeDtypeStruct(s, t) for s, t in shapes],
        in_specs=in_specs,
        out_specs=[VMEM] * len(shapes),
        scratch_shapes=scratch,
        cost_estimate=pl.CostEstimate(flops=flops, bytes_accessed=4 << 20, transcendentals=0),
        compiler_params=pltpu.CompilerParams(vmem_limit_bytes=40 << 20),
    )


def stack(a_ref, b_ref, a_rows, b_rows):
    a, b = a_ref[:, a_rows], b_ref[:, b_rows]
    return jnp.concatenate([a.reshape(-1, a.shape[2]), b.reshape(-1, b.shape[2])], axis=0)


def hidden_kernel(
    xa, yb, a_ref, b_ref, gate_ref, up_ref, down_ref, prob_ref,
    dx_ref, pair_ref, scaled_ref, score_ref,
):
    units = gate_ref.shape[1]
    x_t = stack(a_ref, b_ref, slice(0, xa), slice(yb, None))
    gate = dot(gate_ref[...], x_t, 0, 0)
    up = dot(up_ref[...], x_t, 0, 0)
    y_t = stack(a_ref, b_ref, slice(xa, None), slice(0, yb))
    back = dot(down_ref[...], y_t, 1, 0)
    prob = prob_ref[...]
    sig = jax.nn.sigmoid(gate)
    swish = gate * sig
    hidden = swish * up
    scaled_ref[...] = (prob * hidden).astype(BF)
    score_ref[...] = jnp.sum(hidden.astype(BF).astype(F32) * back, axis=0, keepdims=True)
    scaled_back = prob * back
    pair_ref[:units] = (scaled_back * up * sig * (1.0 + gate * (1.0 - sig))).astype(BF)
    pair_ref[units:] = (scaled_back * swish).astype(BF)
    pair = pair_ref[...]
    step = dx_ref.shape[0] // 8
    for i in range(8):
        at = slice(i * step, (i + 1) * step)
        both = jnp.concatenate([gate_ref[at], up_ref[at]], axis=1)
        dx_ref[at] = dot(both, pair, 1, 0).astype(BF)


def weight_kernel(xa, yb, core_ref, a_ref, b_ref, pair_ref, scaled_ref, away_ref, kept_ref, y_ref):
    units = scaled_ref.shape[0]
    y_ref[...] = stack(a_ref, b_ref, slice(xa, None), slice(0, yb))
    pair, scaled = pair_ref[...], scaled_ref[...]
    quarter = y_ref.shape[0] // 4
    lines = quarter // xa
    core = core_ref[0]
    for half in range(2):
        source, rows = (a_ref, slice(0, xa)) if half == 0 else (b_ref, slice(yb, None))
        for out_ref, which in ((away_ref, 1 - core), (kept_ref, core)):
            x_t = source[pl.ds(which * lines, lines), rows].reshape(quarter, -1)
            grads = dot(x_t, pair, 1, 1)
            out_ref[half, :quarter] = grads[:, :units].astype(BF)
            out_ref[half, quarter : 2 * quarter] = grads[:, units:].astype(BF)
            start = pl.multiple_of((2 * half + which) * quarter, quarter)
            down = dot(scaled, y_ref[pl.ds(start, quarter)], 1, 1).astype(BF)
            for q in range(quarter // units):
                at = 2 * quarter + q * units
                out_ref[half, at : at + units] = down[:, q * units : (q + 1) * units]


def return_kernel(feats, parts_ref, target_ref, score_ref, out_ref):
    own_dx = jnp.sum(parts_ref[...].astype(F32), axis=0).astype(BF)
    rows = own_dx.shape[1]
    owned = target_ref.shape[1]
    score = score_ref[...]
    high = score.astype(BF).astype(F32)
    low = score - high
    blank = jnp.zeros((feats, rows), BF)
    line = lax.broadcasted_iota(jnp.int32, (owned * feats, rows), 0)
    row = lax.broadcasted_iota(jnp.int32, (target_ref.shape[0], rows), 1)
    total = 0.0
    for j in range(owned):
        tail = jnp.where(line == 2 * j, high, jnp.where(line == 2 * j + 1, low, 0.0)).astype(BF)
        laid = [own_dx if i == j else blank for i in range(owned)] + [tail]
        pick = jnp.where(row == target_ref[:, j : j + 1], 1.0, 0.0).astype(BF)
        total = total + dot(pick, jnp.concatenate(laid, axis=0), 1, 1)
    out_ref[...] = total.astype(BF)


def sum_kernel(scores_ref, kept_ref, far_ref, gate_ref, up_ref, down_ref):
    del scores_ref
    quarter, units = gate_ref.shape[1:]
    total = (kept_ref[...] + far_ref[...].astype(F32)).astype(BF)
    gate_ref[0] = total[:quarter]
    up_ref[0] = total[quarter : 2 * quarter]
    for q in range(quarter // units):
        at = 2 * quarter + q * units
        down_ref[0, :, q * units : (q + 1) * units] = total[at : at + units]


def shards(
    tokens, cotangent, expert_ids, slot_ids, route_probs, gate_weight, up_weight, down_weight
):
    peers = lax.axis_size("fsdp")
    experts = lax.axis_size("expert")
    mine = lax.axis_index("expert")
    owned, _, width = tokens.shape
    feats = width // peers
    capacity = 2 * expert_ids.shape[0] // experts
    rows = experts * capacity
    units = gate_weight.shape[2]

    side = 1
    while side * side < peers:
        side *= 2
    xa, ya, xb, yb = feats * 4 * side // 8, feats * 3 * side // 8, feats * 4 * side // 8, feats * 5 * side // 8
    in_row = [[i * side + j for j in range(side)] for i in range(side)]
    in_column = [[i * side + j for i in range(side)] for j in range(side)]

    fields = [expert_ids[:, 0, :].astype(BF), slot_ids[:, 0, :].astype(BF), route_probs[:, 0, :]]
    fields = jnp.concatenate(fields, axis=1).reshape(peers, owned * 6)

    own_x, own_y = tokens[:, 0, :], cotangent[:, 0, :]
    full = (owned, side, side)
    a_x = own_x[:, : side * xa].reshape(owned, 1, side, xa)
    a_y = own_y[:, : side * ya].reshape(owned, 1, side, ya)
    b_y = own_y[:, side * ya :].reshape(owned, side, 1, yb)
    b_x = own_x[:, side * xa :].reshape(owned, side, 1, xb)
    cut = [jnp.broadcast_to(v, full + v.shape[3:]) for v in (a_x, a_y, b_y, b_x)]
    cut = jnp.concatenate(cut, axis=3).transpose(1, 2, 0, 3)
    part = xa + ya + xb + yb
    block = cut.reshape(peers, owned * part // 128, 128)
    block = jnp.broadcast_to(block[None], (experts,) + block.shape)
    block = block.reshape((experts * peers,) + block.shape[2:])
    got = lax.all_to_all(block, ("expert", "fsdp"), 0, 0, tiled=True)
    shifts = [fields] + [
        lax.ppermute(fields, "expert", [(i, (i + d) % experts) for i in range(experts)])
        for d in range(1, experts)
    ]
    turned = jnp.concatenate(shifts[::-1] + shifts[:0:-1], axis=0)
    got_route = lax.dynamic_slice_in_dim(
        turned, (experts - 1 - mine) * peers, experts * peers, 0
    ).astype(F32)
    got_cut = got.reshape(experts * peers, owned, part)

    source = lax.broadcasted_iota(jnp.int32, (peers * experts, 1), 0) // peers * capacity
    row_iota = lax.broadcasted_iota(jnp.int32, (peers * experts, rows), 1)
    targets, prob_row, cut_t = [], 0.0, 0.0
    for j in range(owned):
        first_at = 6 * j
        route = got_route[:, first_at : first_at + 6]
        first = jnp.logical_and(route[:, 0:1] == mine.astype(F32), route[:, 2:3] >= 0)
        second = jnp.logical_and(route[:, 1:2] == mine.astype(F32), route[:, 3:4] >= 0)
        slot = jnp.where(first, route[:, 2:3], route[:, 3:4]).astype(jnp.int32)
        target = jnp.where(jnp.logical_or(first, second), source + slot, -1)
        pick = row_iota == target
        prob = jnp.where(first, route[:, 4:5], route[:, 5:6])
        prob_row = prob_row + jnp.sum(jnp.where(pick, prob, 0.0), axis=0, keepdims=True)
        targets.append(target)
        cut_t = cut_t + dot(got_cut[:, j], pick.astype(BF), 0, 0)
    cut_t = cut_t.astype(BF)
    a_cut, b_cut = cut_t[: xa + ya], cut_t[xa + ya :]
    b_cut = jnp.broadcast_to(b_cut[None], (side,) + b_cut.shape)
    b_full = lax.all_to_all(b_cut, "fsdp", 0, 0, axis_index_groups=in_column, tiled=True)
    a_full = lax.all_gather(a_cut, "fsdp", axis=0, axis_index_groups=in_row)
    a_full, b_full = a_full.reshape(side, xa + ya, rows), b_full.reshape(side, xb + yb, rows)
    dx, pair, scaled, score = call(
        functools.partial(hidden_kernel, xa, yb),
        [((width, rows), BF), ((2 * units, rows), BF), ((units, rows), BF), ((1, rows), F32)],
        [VMEM] * 6,
        flops=10 * width * units * rows,
    )(a_full, b_full, gate_weight[0], up_weight[0], down_weight[0], prob_row)

    parts = lax.all_to_all(dx.reshape(peers, feats, rows), "fsdp", 0, 0, tiled=True)

    quarter = width // 4
    dp = lax.axis_index("dp")
    core, half = dp % 2, dp // 2
    away, kept = call(
        functools.partial(weight_kernel, xa, yb),
        [((2, 3 * quarter, units), BF)] * 2,
        [SMEM] + [VMEM] * 4,
        [pltpu.VMEM((width, rows), BF)],
        flops=6 * width * units * rows,
    )(core[None], a_full, b_full, pair, scaled)
    near = lax.ppermute(away, "dp", [(0, 1), (1, 0), (2, 3), (3, 2)])
    both = kept.astype(F32) + near.astype(F32)
    away = lax.dynamic_index_in_dim(both, 1 - half, 0, keepdims=False).astype(BF)
    kept = lax.dynamic_index_in_dim(both, half, 0, keepdims=False)
    far = lax.ppermute(away, "dp", [(0, 2), (2, 0), (1, 3), (3, 1)])

    (returned,) = call(
        functools.partial(return_kernel, feats),
        [((experts * peers, 2 * owned * feats), BF)],
        [VMEM] * 3,
    )(parts, jnp.concatenate(targets, axis=1), score)
    home = lax.all_to_all(returned, ("expert", "fsdp"), 0, 0, tiled=True)
    home = home.astype(F32).reshape(experts, peers, 2 * owned * feats)
    token_grad = jnp.sum(home[:, :, : owned * feats], axis=0).astype(BF)
    token_grad = token_grad.reshape(peers, owned, feats).transpose(1, 0, 2).reshape(owned, 1, width)
    scores = jnp.sum(home[:, :, owned * feats : owned * feats + 2 * owned], axis=1)
    scores = scores.reshape(experts, owned, 2).sum(axis=2)
    me = lax.axis_index("fsdp")
    own_ids = lax.dynamic_slice_in_dim(expert_ids[:, 0, :], me * owned, owned, 0)
    own_slots = lax.dynamic_slice_in_dim(slot_ids[:, 0, :], me * owned, owned, 0)
    expert_iota = lax.broadcasted_iota(jnp.int32, (experts, owned, 2), 0)
    chosen = jnp.logical_and(expert_iota == own_ids[None], own_slots[None] >= 0)
    prob_grad = jnp.sum(jnp.where(chosen, scores[:, :, None], 0.0), axis=0)
    grad_gate, grad_up, grad_down = call(
        sum_kernel,
        [((1, quarter, units), BF)] * 2 + [((1, units, quarter), BF)],
        [pl.BlockSpec(memory_space=pl.ANY)] + [VMEM] * 2,
    )(scores, kept, far)
    return grad_gate, grad_up, grad_down, token_grad, prob_grad[:, None, :]


def solution(mesh):
    return jax.shard_map(
        shards,
        mesh=mesh,
        in_specs=(
            P("fsdp", ("expert", "dp"), None),
            P("fsdp", ("expert", "dp"), None),
            P(None, ("expert", "dp"), None),
            P(None, ("expert", "dp"), None),
            P(None, ("expert", "dp"), None),
            P("expert", None, "fsdp"),
            P("expert", None, "fsdp"),
            P("expert", "fsdp", None),
        ),
        out_specs=(
            P("expert", "dp", "fsdp"),
            P("expert", "dp", "fsdp"),
            P("expert", "fsdp", "dp"),
            P("fsdp", ("expert", "dp"), None),
            P("fsdp", ("expert", "dp"), None),
        ),
        check_vma=False,
    )
```

time: 177 us -> 157 us (0.89)
  blocking collectives: 40.8 us -> 25.9 us
  local copies, waits for them, and re-layouts: 18.2 us -> 11.7 us
  matrix products: 5.65 us -> 0.6 us
  Pallas kernels: 0 us -> 4.09 us
  waiting for transfers between devices: 37.7 us -> 41.3 us
    all_gather x1 -> x0, blocking collectives: 14.5 us -> none  [shards(): got_route = lax.all_gather(fields, 'expert', axis=0, tiled=True).astype(F32)]
    ppermute x0 -> x3, starting transfers between devices: none -> 10.9 us  [shards(): lax.ppermute(fields, 'expert', [(i, (i + d) % experts) for i in range(exp...]
    all_to_all x1, starting transfers between devices: 18.2 us -> 8.91 us  [shards(): home = lax.all_to_all(returned, ('expert', 'fsdp'), 0, 0, tiled=True)]
    ppermute x1, waiting for transfers between devices: 5.32 us -> 0.01 us  [shards(): far = lax.ppermute(away, 'dp', [(0, 2), (2, 0), (1, 3), (3, 1)])]
    dot_general x12 -> x2, matrix products: 5.65 us -> 0.6 us  [dot(): lax.dot_general(a, b, (((ca,), (cb,)), ((), ())), preferred_element_type=...]
    ppermute x0 -> x3, waiting for transfers between devices: none -> 4.75 us  [shards(): lax.ppermute(fields, 'expert', [(i, (i + d) % experts) for i in range(exp...]
    pallas_call x0 -> x4, Pallas kernels: none -> 4.09 us  [the longest x1 1.58 us: shards(): call(functools.partial(weight_kernel, xa, yb), [((2, 3 * quarter, units),...]
    ppermute x1, waiting for transfers between devices: 0.01 us -> 1.93 us  [shards(): near = lax.ppermute(away, 'dp', [(0, 1), (1, 0), (2, 3), (3, 2)])]
  transfers between devices with their start and end apart: 6 -> 9, of which waited for: 5 -> 7; matrix products, arithmetic and copies ran while one was open for 8% -> 4% of each run, Pallas kernels for 0% -> 1%
where the time goes in v3:
time: 157 us; the launch traced here: 156 us
  starting transfers between devices  68.6 us (44%)
  waiting for transfers between devices  41.3 us (26%)
  blocking collectives  25.9 us (16%)
  local copies, waits for them, and re-layouts  11.7 us (7%)
  Pallas kernels  4.09 us (3%)
  other arithmetic  3.27 us (2%)
    all_to_all x1, starting transfers between devices, shards(): got = lax.all_to_all(block, ('expert', 'fsdp'), 0, 0, tiled=True)  28.4 us
    all_gather x1, blocking collectives, shards(): a_full = lax.all_gather(a_cut, 'fsdp', axis=0, axis_index_groups=in_row)  25.9 us
    all_to_all x1, waiting for transfers between devices, shards(): home = lax.all_to_all(returned, ('expert', 'fsdp'), 0, 0, tiled=True)  14.3 us
    all_to_all x1, waiting for transfers between devices, shards(): lax.all_to_all(dx.reshape(peers, feats, rows), 'fsdp', 0, 0, tiled=True)  12.4 us
    ppermute x3, starting transfers between devices, shards(): lax.ppermute(fields, 'expert', [(i, (i + d) % experts) for i in range(exp...  10.9 us
    all_to_all x1, starting transfers between devices, shards(): lax.all_to_all(dx.reshape(peers, feats, rows), 'fsdp', 0, 0, tiled=True)  9.18 us
    all_to_all x1, starting transfers between devices, shards(): home = lax.all_to_all(returned, ('expert', 'fsdp'), 0, 0, tiled=True)  8.91 us
    ppermute x1, starting transfers between devices, shards(): far = lax.ppermute(away, 'dp', [(0, 2), (2, 0), (1, 3), (3, 1)])  5.47 us
  transfers between devices with their start and end apart: 9, of which 7 were waited for; matrix products, arithmetic and copies ran while one was open for 4% of the time, Pallas kernels for 1%

profile of v3, /device:TPU:2, one launch (start us, length us, event | category | flops | bytes accessed | tf_op | source)
XLA Modules:
  0.0 156.5 jit_solution(7016870376231592102)
XLA Ops:
  0.7 0.7 slice.108
  1.4 0.7 slice.107
  2.1 0.7 slice_bitcast_fusion.5
  3.1 0.2 maximum_bitcast_fusion
  3.4 0.9 broadcast_in_dim.98
  4.3 28.4 %all-to-all-start = ((bf16[256,8,128]{2,1,0:T(8,128)(2,1)}), bf16[256,8,128]{2,1,0:T(8,128)(2,1)S(1)}, u32[]{:S(2)}, u32[]{:S(2)}) async-start(bf16[256,8,128]{2,1,0:T(8,128)(2,1)} %bitcast.5), calls=%async_computation | async-start | bytes 1048576 | tf_op jit(solution)/shard_map/all_to_all | solution.py:151
  32.7 0.1 copy.81
  32.9 6.4 %collective-permute-start = (bf16[64,12]{1,0:T(8,128)(2,1)S(1)}, bf16[64,12]{1,0:T(8,128)(2,1)S(1)}, u32[]{:S(2)}, u32[]{:S(2)}) collective-permute-start(bf16[64,12]{1,0:T(8,128)(2,1)S(1)} %reshape.142), channel_id=1, source_target_pairs={{0,12},{4,0},{8,4},{12,8},{1,13},{5,1},{9,5},{13,9},{2,14},{6,2},{... | collective-permute-start | bytes 4616 | tf_op jit(solution)/shard_map/ppermute | solution.py:153
  39.3 1.9 %collective-permute-start.1 = (bf16[64,12]{1,0:T(8,128)(2,1)S(1)}, bf16[64,12]{1,0:T(8,128)(2,1)S(1)}, u32[]{:S(2)}, u32[]{:S(2)}) collective-permute-start(bf16[64,12]{1,0:T(8,128)(2,1)S(1)} %reshape.142), channel_id=1, source_target_pairs={{0,8},{4,12},{8,0},{12,4},{1,9},{5,13},{9,1},{13,5},{2,10},{6,14},... | collective-permute-start | bytes 4616 | tf_op jit(solution)/shard_map/ppermute | solution.py:153
  41.2 2.6 %collective-permute-start.2 = (bf16[64,12]{1,0:T(8,128)(2,1)S(1)}, bf16[64,12]{1,0:T(8,128)(2,1)S(1)}, u32[]{:S(2)}, u32[]{:S(2)}) collective-permute-start(bf16[64,12]{1,0:T(8,128)(2,1)S(1)} %reshape.142), channel_id=1, source_target_pairs={{0,4},{4,8},{8,12},{12,0},{1,5},{5,9},{9,13},{13,1},{2,6},{6,10},{... | collective-permute-start | bytes 4616 | tf_op jit(solution)/shard_map/ppermute | solution.py:153
  44.0 2.2 %collective-permute-done.1 = bf16[64,12]{1,0:T(8,128)(2,1)S(1)} collective-permute-done((bf16[64,12]{1,0:T(8,128)(2,1)S(1)}, bf16[64,12]{1,0:T(8,128)(2,1)S(1)}, u32[]{:S(2)}, u32[]{:S(2)}) %collective-permute-start.1) | collective-permute-done | bytes 1568 | tf_op jit(solution)/shard_map/ppermute | solution.py:153
  46.3 2.5 %collective-permute-done.2 = bf16[64,12]{1,0:T(8,128)(2,1)S(1)} collective-permute-done((bf16[64,12]{1,0:T(8,128)(2,1)S(1)}, bf16[64,12]{1,0:T(8,128)(2,1)S(1)}, u32[]{:S(2)}, u32[]{:S(2)}) %collective-permute-start.2) | collective-permute-done | bytes 1568 | tf_op jit(solution)/shard_map/ppermute | solution.py:153
  48.9 0.1 concatenate.14
  49.1 4.7 %all-to-all-done = bf16[256,8,128]{2,1,0:T(8,128)(2,1)S(1)} async-done(((bf16[256,8,128]{2,1,0:T(8,128)(2,1)}), bf16[256,8,128]{2,1,0:T(8,128)(2,1)S(1)}, u32[]{:S(2)}, u32[]{:S(2)}) %all-to-all-start) | async-done | bytes 524320 | tf_op jit(solution)/shard_map/all_to_all | solution.py:151
  53.8 0.3 copy.79
  54.1 0.3 fusion.2
  54.4 0.3 fusion
  54.7 1.1 broadcast_in_dim.99
  55.8 3.9 %all-to-all-start.1 = ((bf16[8,288,256]{2,1,0:T(8,128)(2,1)}), bf16[8,288,256]{2,1,0:T(8,128)(2,1)S(1)}, u32[]{:S(2)}, u32[]{:S(2)}) async-start(bf16[8,288,256]{2,1,0:T(8,128)(2,1)} %broadcast_in_dim.99), calls=%async_computation.1 | async-start | bytes 2359296 | tf_op jit(solution)/shard_map/all_to_all | solution.py:180
  59.8 0.1 select_reduce_fusion.1
  59.9 0.1 select_reduce_fusion
  60.1 25.9 %all-gather = bf16[1792,256]{1,0:T(8,128)(2,1)S(1)} all-gather(bf16[224,256]{1,0:T(8,128)(2,1)S(1)} %slice.120), channel_id=2, replica_groups={{0,16,32,48,64,80,96,112},{128,144,160,176,192,208,224,240},{256,272,28..., dimensions={0}, use_global_device_ids=true | all-gather | bytes 1032192 | tf_op jit(solution)/shard_map/all_gather | solution.py:181
  86.0 3.3 %all-to-all-done.1.b_ref = bf16[8,288,256]{2,1,0:T(8,128)(2,1)S(1)} async-done(((bf16[8,288,256]{2,1,0:T(8,128)(2,1)}), bf16[8,288,256]{2,1,0:T(8,128)(2,1)S(1)}, u32[]{:S(2)}, u32[]{:S(2)}) %all-to-all-start.1) | async-done | bytes 1179680 | tf_op jit(solution)/shard_map/all_to_all | solution.py:180
  89.3 1.0 copy-done.4
  90.4 1.3 shard_map.119
  91.7 1.0 copy-done
  92.7 9.2 %all-to-all-start.2 = ((bf16[64,32,256]{2,1,0:T(8,128)(2,1)}), bf16[64,32,256]{2,1,0:T(8,128)(2,1)S(1)}, u32[]{:S(2)}, u32[]{:S(2)}) async-start(bf16[64,32,256]{2,1,0:T(8,128)(2,1)} %bitcast.51), calls=%async_computation.2 | async-start | bytes 2097152 | tf_op jit(solution)/shard_map/all_to_all | solution.py:190
  101.9 1.6 %shard_map.121 = (bf16[2,1536,128]{2,1,0:T(8,128)(2,1)}, bf16[2,1536,128]{2,1,0:T(8,128)(2,1)S(1)}) custom-call(s32[1]{0:T(128)} %bitcast.25.core_ref, bf16[8,224,256]{2,1,0:T(8,128)(2,1)S(1)} %bitcast.50, bf16[8,288,256]{2,1,0:T(8,128)(2,1)S(1)} %all-to-all-done.1.b_ref, bf16[256,256]{1,0:T(8,128)(2,1)S(1)} %get-tuple-element.16.pair_ref, ...), custom_call_target="tpu_custom_call" | custom-call | flops 402653184 | bytes 4194304 | tf_op jit(solution)/shard_map/pallas_call | solution.py:195
  103.4 0.9 copy-done.1
  104.4 1.9 %collective-permute-start.3 = (bf16[2,1536,128]{2,1,0:T(8,128)(2,1)}, bf16[2,1536,128]{2,1,0:T(8,128)(2,1)S(1)}, u32[]{:S(2)}, u32[]{:S(2)}) collective-permute-start(bf16[2,1536,128]{2,1,0:T(8,128)(2,1)} %get-tuple-element.19), channel_id=1, source_target_pairs={{0,1},{1,0},{2,3},{3,2},{4,5},{5,4},{6,7},{7,6},{8,9},{9,8},{10,11... | collective-permute-start | bytes 2359304 | tf_op jit(solution)/shard_map/ppermute | solution.py:202
  106.4 0.1 copy.97
  106.6 0.1 copy.96
  106.7 0.1 copy.90.target_ref
  106.8 1.9 %collective-permute-done.3 = bf16[2,1536,128]{2,1,0:T(8,128)(2,1)S(1)} collective-permute-done((bf16[2,1536,128]{2,1,0:T(8,128)(2,1)}, bf16[2,1536,128]{2,1,0:T(8,128)(2,1)S(1)}, u32[]{:S(2)}, u32[]{:S(2)}) %collective-permute-start.3) | collective-permute-done | bytes 786464 | tf_op jit(solution)/shard_map/ppermute | solution.py:202
  108.7 0.9 copy-done.5
  109.6 1.5 convert_add_fusion
  111.2 5.5 %collective-permute-start.4 = (bf16[1536,128]{1,0:T(8,128)(2,1)S(1)}, bf16[1536,128]{1,0:T(8,128)(2,1)S(1)}, u32[]{:S(2)}, u32[]{:S(2)}) collective-permute-start(bf16[1536,128]{1,0:T(8,128)(2,1)S(1)} %fusion.1), channel_id=1, source_target_pairs={{0,2},{2,0},{1,3},{3,1},{4,6},{6,4},{5,7},{7,5},{8,10},{10,8},{9,1... | collective-permute-start | bytes 1179656 | tf_op jit(solution)/shard_map/ppermute | solution.py:206
  116.7 12.4 %all-to-all-done.2.parts_ref = bf16[64,32,256]{2,1,0:T(8,128)(2,1)S(1)} async-done(((bf16[64,32,256]{2,1,0:T(8,128)(2,1)}), bf16[64,32,256]{2,1,0:T(8,128)(2,1)S(1)}, u32[]{:S(2)}, u32[]{:S(2)}) %all-to-all-start.2) | async-done | bytes 1048608 | tf_op jit(solution)/shard_map/all_to_all | solution.py:190
  129.1 0.4 shard_map.120
  129.5 0.8 copy.91
  130.2 8.9 %all-to-all-start.3 = ((bf16[256,1,128]{2,1,0:T(2,128)(2,1)}), bf16[256,1,128]{2,1,0:T(2,128)(2,1)S(1)}, u32[]{:S(2)}, u32[]{:S(2)}) async-start(bf16[256,1,128]{2,1,0:T(2,128)(2,1)} %copy.91), calls=%async_computation.3 | async-start | bytes 262144 | tf_op jit(solution)/shard_map/all_to_all | solution.py:213
  139.2 14.3 %all-to-all-done.3 = bf16[256,1,128]{2,1,0:T(2,128)(2,1)S(1)} async-done(((bf16[256,1,128]{2,1,0:T(2,128)(2,1)}), bf16[256,1,128]{2,1,0:T(2,128)(2,1)S(1)}, u32[]{:S(2)}, u32[]{:S(2)}) %all-to-all-start.3) | async-done | bytes 65568 | tf_op jit(solution)/shard_map/all_to_all | solution.py:213
  153.5 0.1 convert_element_type.75
  153.7 0.1 slice_reduce_fusion.1
  154.1 0.1 copy.95
  154.2 0.7 reshape.145
  154.9 0.7 fusion.5
  155.7 0.8 shard_map.122
  (48 shorter events, 1.6 us)
Async XLA Ops:
  0.6 32.0 %copy-start.6 = (s32[128,1,2]{0,2,1:T(2,128)S(1)}, s32[128,1,2]{0,2,1:T(2,128)}, u32[]{:S(2)}) copy-start(s32[128,1,2]{0,2,1:T(2,128)} %param.11) | copy-start | bytes 3076
  0.6 32.0 %copy-start.7 = (s32[128,1,2]{0,2,1:T(2,128)S(1)}, s32[128,1,2]{0,2,1:T(2,128)}, u32[]{:S(2)}) copy-start(s32[128,1,2]{0,2,1:T(2,128)} %param.10) | copy-start | bytes 3076
  0.7 32.0 %copy-start.8 = (bf16[128,1,2]{0,2,1:T(2,128)(2,1)S(1)}, bf16[128,1,2]{0,2,1:T(2,128)(2,1)}, u32[]{:S(2)}) copy-start(bf16[128,1,2]{0,2,1:T(2,128)(2,1)} %param.12) | copy-start | bytes 1540
  4.3 49.5 %all-to-all-start = ((bf16[256,8,128]{2,1,0:T(8,128)(2,1)}), bf16[256,8,128]{2,1,0:T(8,128)(2,1)S(1)}, u32[]{:S(2)}, u32[]{:S(2)}) async-start(bf16[256,8,128]{2,1,0:T(8,128)(2,1)} %bitcast.5), calls=%async_computation | async-start | bytes 1048576 | tf_op jit(solution)/shard_map/all_to_all | solution.py:151
  32.9 11.0 %collective-permute-start = (bf16[64,12]{1,0:T(8,128)(2,1)S(1)}, bf16[64,12]{1,0:T(8,128)(2,1)S(1)}, u32[]{:S(2)}, u32[]{:S(2)}) collective-permute-start(bf16[64,12]{1,0:T(8,128)(2,1)S(1)} %reshape.142), channel_id=1, source_target_pairs={{0,12},{4,0},{8,4},{12,8},{1,13},{5,1},{9,5},{13,9},{2,14},{6,2},{... | collective-permute-start | bytes 4616 | tf_op jit(solution)/shard_map/ppermute | solution.py:153
  39.3 6.9 %collective-permute-start.1 = (bf16[64,12]{1,0:T(8,128)(2,1)S(1)}, bf16[64,12]{1,0:T(8,128)(2,1)S(1)}, u32[]{:S(2)}, u32[]{:S(2)}) collective-permute-start(bf16[64,12]{1,0:T(8,128)(2,1)S(1)} %reshape.142), channel_id=1, source_target_pairs={{0,8},{4,12},{8,0},{12,4},{1,9},{5,13},{9,1},{13,5},{2,10},{6,14},... | collective-permute-start | bytes 4616 | tf_op jit(solution)/shard_map/ppermute | solution.py:153
  41.2 7.6 %collective-permute-start.2 = (bf16[64,12]{1,0:T(8,128)(2,1)S(1)}, bf16[64,12]{1,0:T(8,128)(2,1)S(1)}, u32[]{:S(2)}, u32[]{:S(2)}) collective-permute-start(bf16[64,12]{1,0:T(8,128)(2,1)S(1)} %reshape.142), channel_id=1, source_target_pairs={{0,4},{4,8},{8,12},{12,0},{1,5},{5,9},{9,13},{13,1},{2,6},{6,10},{... | collective-permute-start | bytes 4616 | tf_op jit(solution)/shard_map/ppermute | solution.py:153
  55.8 33.5 %copy-start.2 = (bf16[1,2048,128]{2,1,0:T(8,128)(2,1)S(1)}, bf16[1,2048,128]{2,1,0:T(8,128)(2,1)}, u32[]{:S(2)}) copy-start(bf16[1,2048,128]{2,1,0:T(8,128)(2,1)} %param.13) | copy-start | bytes 1572868
  55.8 33.5 %copy-start.3 = (bf16[1,2048,128]{2,1,0:T(8,128)(2,1)S(1)}, bf16[1,2048,128]{2,1,0:T(8,128)(2,1)}, u32[]{:S(2)}) copy-start(bf16[1,2048,128]{2,1,0:T(8,128)(2,1)} %param.14) | copy-start | bytes 1572868
  55.8 33.5 %all-to-all-start.1 = ((bf16[8,288,256]{2,1,0:T(8,128)(2,1)}), bf16[8,288,256]{2,1,0:T(8,128)(2,1)S(1)}, u32[]{:S(2)}, u32[]{:S(2)}) async-start(bf16[8,288,256]{2,1,0:T(8,128)(2,1)} %broadcast_in_dim.99), calls=%async_computation.1 | async-start | bytes 2359296 | tf_op jit(solution)/shard_map/all_to_all | solution.py:180
  89.3 1.0 copy-start.4
  91.7 1.0 copy-start
  92.7 36.4 %all-to-all-start.2 = ((bf16[64,32,256]{2,1,0:T(8,128)(2,1)}), bf16[64,32,256]{2,1,0:T(8,128)(2,1)S(1)}, u32[]{:S(2)}, u32[]{:S(2)}) async-start(bf16[64,32,256]{2,1,0:T(8,128)(2,1)} %bitcast.51), calls=%async_computation.2 | async-start | bytes 2097152 | tf_op jit(solution)/shard_map/all_to_all | solution.py:190
  103.4 0.9 copy-start.1
  104.4 4.4 %collective-permute-start.3 = (bf16[2,1536,128]{2,1,0:T(8,128)(2,1)}, bf16[2,1536,128]{2,1,0:T(8,128)(2,1)S(1)}, u32[]{:S(2)}, u32[]{:S(2)}) collective-permute-start(bf16[2,1536,128]{2,1,0:T(8,128)(2,1)} %get-tuple-element.19), channel_id=1, source_target_pairs={{0,1},{1,0},{2,3},{3,2},{4,5},{5,4},{6,7},{7,6},{8,9},{9,8},{10,11... | collective-permute-start | bytes 2359304 | tf_op jit(solution)/shard_map/ppermute | solution.py:202
  108.7 0.9 copy-start.5
  111.2 44.4 %collective-permute-start.4 = (bf16[1536,128]{1,0:T(8,128)(2,1)S(1)}, bf16[1536,128]{1,0:T(8,128)(2,1)S(1)}, u32[]{:S(2)}, u32[]{:S(2)}) collective-permute-start(bf16[1536,128]{1,0:T(8,128)(2,1)S(1)} %fusion.1), channel_id=1, source_target_pairs={{0,2},{2,0},{1,3},{3,1},{4,6},{6,4},{5,7},{7,5},{8,10},{10,8},{9,1... | collective-permute-start | bytes 1179656 | tf_op jit(solution)/shard_map/ppermute | solution.py:206
  130.2 23.3 %all-to-all-start.3 = ((bf16[256,1,128]{2,1,0:T(2,128)(2,1)}), bf16[256,1,128]{2,1,0:T(2,128)(2,1)S(1)}, u32[]{:S(2)}, u32[]{:S(2)}) async-start(bf16[256,1,128]{2,1,0:T(2,128)(2,1)} %copy.91), calls=%async_computation.3 | async-start | bytes 262144 | tf_op jit(solution)/shard_map/all_to_all | solution.py:213

commit v4 on v3

--- a/solution.py
+++ b/solution.py
@@ -17,6 +17,10 @@
 
 VMEM = pl.BlockSpec(memory_space=pltpu.VMEM)
 SMEM = pl.BlockSpec(memory_space=pltpu.SMEM)
+
+
+ANY = pl.BlockSpec(memory_space=pl.ANY)
+HBM = pl.BlockSpec(memory_space=pltpu.HBM)
 
 
 def call(kernel, shapes, in_specs, scratch=(), flops=0):
@@ -29,6 +33,48 @@
         cost_estimate=pl.CostEstimate(flops=flops, bytes_accessed=4 << 20, transcendentals=0),
         compiler_params=pltpu.CompilerParams(vmem_limit_bytes=40 << 20),
     )
+
+
+def send_kernel(side, ya, yb, x_ref, y_ref, out_ref, block_ref, sems):
+    x, y = x_ref[...].astype(F32), y_ref[...].astype(F32)
+    owned, lanes = x.shape[0], block_ref.shape[2]
+    lane = lax.broadcasted_iota(jnp.int32, (owned, lanes), 1)
+    none = jnp.zeros((owned, lanes), F32)
+
+    def tile(lines):
+        return jnp.concatenate([v[t : t + 1] for t in range(owned) for v in lines], axis=0)
+
+    by_x, by_z = [], []
+    for i in range(side):
+        head = jnp.where(lane < ya, y[:, i * ya : i * ya + lanes], 0.0)
+        by_x.append(tile([x[:, i * lanes : (i + 1) * lanes], head, none, none]))
+        at = side * ya + i * yb
+        middle = jnp.where(lane >= ya, y[:, at - ya : at - ya + lanes], 0.0)
+        last = y[:, at + lanes - ya : at + 2 * lanes - ya]
+        at = (side + i) * lanes
+        by_z.append(tile([none, middle, last, x[:, at : at + lanes]]))
+    for i in range(side):
+        for j in range(side):
+            block_ref[i * side + j] = (by_z[i] + by_x[j]).astype(BF)
+    copies = [
+        pltpu.make_async_copy(block_ref, out_ref.at[k], sems.at[k]) for k in range(out_ref.shape[0])
+    ]
+    for copy in copies:
+        copy.start()
+    for copy in copies:
+        copy.wait()
+
+
+def lay_out(own_x, own_y, experts, side, ya, yb):
+    shape = (side * side, own_x.shape[0] * 4, 128)
+    return pl.pallas_call(
+        functools.partial(send_kernel, side, ya, yb),
+        out_shape=jax.ShapeDtypeStruct((experts,) + shape, BF),
+        in_specs=[VMEM] * 2,
+        out_specs=HBM,
+        scratch_shapes=[pltpu.VMEM(shape, BF), pltpu.SemaphoreType.DMA((experts,))],
+        compiler_params=pltpu.CompilerParams(vmem_limit_bytes=40 << 20),
+    )(own_x, own_y)
 
 
 def stack(a_ref, b_ref, a_rows, b_rows):
@@ -129,24 +175,16 @@
     side = 1
     while side * side < peers:
         side *= 2
-    xa, ya, xb, yb = feats * 4 * side // 8, feats * 3 * side // 8, feats * 4 * side // 8, feats * 5 * side // 8
+    xa = xb = feats * side // 2
+    ya, yb = feats * side * 7 // 16, feats * side * 9 // 16
     in_row = [[i * side + j for j in range(side)] for i in range(side)]
     in_column = [[i * side + j for i in range(side)] for j in range(side)]
 
     fields = [expert_ids[:, 0, :].astype(BF), slot_ids[:, 0, :].astype(BF), route_probs[:, 0, :]]
     fields = jnp.concatenate(fields, axis=1).reshape(peers, owned * 6)
 
-    own_x, own_y = tokens[:, 0, :], cotangent[:, 0, :]
-    full = (owned, side, side)
-    a_x = own_x[:, : side * xa].reshape(owned, 1, side, xa)
-    a_y = own_y[:, : side * ya].reshape(owned, 1, side, ya)
-    b_y = own_y[:, side * ya :].reshape(owned, side, 1, yb)
-    b_x = own_x[:, side * xa :].reshape(owned, side, 1, xb)
-    cut = [jnp.broadcast_to(v, full + v.shape[3:]) for v in (a_x, a_y, b_y, b_x)]
-    cut = jnp.concatenate(cut, axis=3).transpose(1, 2, 0, 3)
     part = xa + ya + xb + yb
-    block = cut.reshape(peers, owned * part // 128, 128)
-    block = jnp.broadcast_to(block[None], (experts,) + block.shape)
+    block = lay_out(tokens[:, 0, :], cotangent[:, 0, :], experts, side, ya, yb)
     block = block.reshape((experts * peers,) + block.shape[2:])
     got = lax.all_to_all(block, ("expert", "fsdp"), 0, 0, tiled=True)
     shifts = [fields] + [
@@ -225,7 +263,7 @@
     grad_gate, grad_up, grad_down = call(
         sum_kernel,
         [((1, quarter, units), BF)] * 2 + [((1, units, quarter), BF)],
-        [pl.BlockSpec(memory_space=pl.ANY)] + [VMEM] * 2,
+        [ANY] + [VMEM] * 2,
     )(scores, kept, far)
     return grad_gate, grad_up, grad_down, token_grad, prob_grad[:, None, :]
 

time: 157 us -> 154 us (0.981)
  waiting for transfers between devices: 41.3 us -> 37.9 us
  local copies, waits for them, and re-layouts: 11.7 us -> 9.69 us
  starting transfers between devices: 68.6 us -> 70.4 us
    broadcast_in_dim x11 -> x0, local copies, waits for them, and re-layouts: 1.95 us -> none  [the longest x9 1.01 us: shards(): jnp.broadcast_to(v, full + v.shape[3:])]
    all_to_all x1, waiting for transfers between devices: 12.4 us -> 10.5 us  [shards(): lax.all_to_all(dx.reshape(peers, feats, rows), 'fsdp', 0, 0, tiled=True)]
    all_to_all x1, waiting for transfers between devices: 3.32 us -> 1.69 us  [shards(): lax.all_to_all(b_cut, 'fsdp', 0, 0, axis_index_groups=in_column, tiled=True)]
    unnamed x18 -> x22, local copies, waits for them, and re-layouts: 3.85 us -> 5.26 us
where the time goes in v4:
time: 154 us
  starting transfers between devices  70.4 us (46%)
  waiting for transfers between devices  37.9 us (25%)
  blocking collectives  26.1 us (17%)
  local copies, waits for them, and re-layouts  9.69 us (6%)
  Pallas kernels  5.05 us (3%)
  other arithmetic  3.05 us (2%)
    all_to_all x1, starting transfers between devices, shards(): got = lax.all_to_all(block, ('expert', 'fsdp'), 0, 0, tiled=True)  28.4 us
    all_gather x1, blocking collectives, shards(): a_full = lax.all_gather(a_cut, 'fsdp', axis=0, axis_index_groups=in_row)  26.1 us
    all_to_all x1, waiting for transfers between devices, shards(): home = lax.all_to_all(returned, ('expert', 'fsdp'), 0, 0, tiled=True)  14.3 us
    ppermute x3, starting transfers between devices, shards(): lax.ppermute(fields, 'expert', [(i, (i + d) % experts) for i in range(exp...  10.9 us
    all_to_all x1, starting transfers between devices, shards(): lax.all_to_all(dx.reshape(peers, feats, rows), 'fsdp', 0, 0, tiled=True)  10.7 us
    all_to_all x1, waiting for transfers between devices, shards(): lax.all_to_all(dx.reshape(peers, feats, rows), 'fsdp', 0, 0, tiled=True)  10.5 us
    all_to_all x1, starting transfers between devices, shards(): home = lax.all_to_all(returned, ('expert', 'fsdp'), 0, 0, tiled=True)  9.1 us
    ppermute x1, starting transfers between devices, shards(): far = lax.ppermute(away, 'dp', [(0, 2), (2, 0), (1, 3), (3, 1)])  5.49 us
  transfers between devices with their start and end apart: 9, of which 7 were waited for; matrix products, arithmetic and copies ran while one was open for 4% of the time, Pallas kernels for 1%

profile of v4, /device:TPU:2, one launch (start us, length us, event | category | flops | bytes accessed | tf_op | source)
XLA Modules:
  0.0 153.8 jit_solution(11464405583667883697)
XLA Ops:
  0.7 0.7 copy-done.5
  1.4 0.7 copy-done.6
  2.1 1.0 shard_map.119
  3.0 28.4 %all-to-all-start = ((bf16[256,8,128]{2,1,0:T(8,128)(2,1)}), bf16[256,8,128]{2,1,0:T(8,128)(2,1)S(1)}, u32[]{:S(2)}, u32[]{:S(2)}) async-start(bf16[256,8,128]{2,1,0:T(8,128)(2,1)} %bitcast.2), calls=%async_computation | async-start | bytes 1048576 | tf_op jit(solution)/shard_map/all_to_all | solution.py:189
  31.5 0.1 copy.53
  31.7 6.4 %collective-permute-start = (bf16[64,12]{1,0:T(8,128)(2,1)S(1)}, bf16[64,12]{1,0:T(8,128)(2,1)S(1)}, u32[]{:S(2)}, u32[]{:S(2)}) collective-permute-start(bf16[64,12]{1,0:T(8,128)(2,1)S(1)} %reshape.133), channel_id=1, source_target_pairs={{0,12},{4,0},{8,4},{12,8},{1,13},{5,1},{9,5},{13,9},{2,14},{6,2},{... | collective-permute-start | bytes 4616 | tf_op jit(solution)/shard_map/ppermute | solution.py:191
  38.1 1.9 %collective-permute-start.1 = (bf16[64,12]{1,0:T(8,128)(2,1)S(1)}, bf16[64,12]{1,0:T(8,128)(2,1)S(1)}, u32[]{:S(2)}, u32[]{:S(2)}) collective-permute-start(bf16[64,12]{1,0:T(8,128)(2,1)S(1)} %reshape.133), channel_id=1, source_target_pairs={{0,8},{4,12},{8,0},{12,4},{1,9},{5,13},{9,1},{13,5},{2,10},{6,14},... | collective-permute-start | bytes 4616 | tf_op jit(solution)/shard_map/ppermute | solution.py:191
  40.0 2.6 %collective-permute-start.2 = (bf16[64,12]{1,0:T(8,128)(2,1)S(1)}, bf16[64,12]{1,0:T(8,128)(2,1)S(1)}, u32[]{:S(2)}, u32[]{:S(2)}) collective-permute-start(bf16[64,12]{1,0:T(8,128)(2,1)S(1)} %reshape.133), channel_id=1, source_target_pairs={{0,4},{4,8},{8,12},{12,0},{1,5},{5,9},{9,13},{13,1},{2,6},{6,10},{... | collective-permute-start | bytes 4616 | tf_op jit(solution)/shard_map/ppermute | solution.py:191
  42.8 2.2 %collective-permute-done.1 = bf16[64,12]{1,0:T(8,128)(2,1)S(1)} collective-permute-done((bf16[64,12]{1,0:T(8,128)(2,1)S(1)}, bf16[64,12]{1,0:T(8,128)(2,1)S(1)}, u32[]{:S(2)}, u32[]{:S(2)}) %collective-permute-start.1) | collective-permute-done | bytes 1568 | tf_op jit(solution)/shard_map/ppermute | solution.py:191
  45.1 2.5 %collective-permute-done.2 = bf16[64,12]{1,0:T(8,128)(2,1)S(1)} collective-permute-done((bf16[64,12]{1,0:T(8,128)(2,1)S(1)}, bf16[64,12]{1,0:T(8,128)(2,1)S(1)}, u32[]{:S(2)}, u32[]{:S(2)}) %collective-permute-start.2) | collective-permute-done | bytes 1568 | tf_op jit(solution)/shard_map/ppermute | solution.py:191
  47.7 0.1 concatenate.10
  47.9 4.7 %all-to-all-done = bf16[256,8,128]{2,1,0:T(8,128)(2,1)S(1)} async-done(((bf16[256,8,128]{2,1,0:T(8,128)(2,1)}), bf16[256,8,128]{2,1,0:T(8,128)(2,1)S(1)}, u32[]{:S(2)}, u32[]{:S(2)}) %all-to-all-start) | async-done | bytes 524320 | tf_op jit(solution)/shard_map/all_to_all | solution.py:189
  52.6 0.3 copy.51
  52.9 0.3 fusion.2
  53.2 0.3 fusion
  53.5 1.1 broadcast_in_dim.54
  54.6 3.9 %all-to-all-start.1 = ((bf16[8,272,256]{2,1,0:T(8,128)(2,1)}), bf16[8,272,256]{2,1,0:T(8,128)(2,1)S(1)}, u32[]{:S(2)}, u32[]{:S(2)}) async-start(bf16[8,272,256]{2,1,0:T(8,128)(2,1)} %broadcast_in_dim.54), calls=%async_computation.1 | async-start | bytes 2228224 | tf_op jit(solution)/shard_map/all_to_all | solution.py:218
  58.5 0.1 select_reduce_fusion.1
  58.7 0.1 select_reduce_fusion
  58.9 26.1 %all-gather = bf16[1920,256]{1,0:T(8,128)(2,1)S(1)} all-gather(bf16[240,256]{1,0:T(8,128)(2,1)S(1)} %slice.100), channel_id=2, replica_groups={{0,16,32,48,64,80,96,112},{128,144,160,176,192,208,224,240},{256,272,28..., dimensions={0}, use_global_device_ids=true | all-gather | bytes 1105920 | tf_op jit(solution)/shard_map/all_gather | solution.py:219
  85.0 1.7 %all-to-all-done.1.b_ref = bf16[8,272,256]{2,1,0:T(8,128)(2,1)S(1)} async-done(((bf16[8,272,256]{2,1,0:T(8,128)(2,1)}), bf16[8,272,256]{2,1,0:T(8,128)(2,1)S(1)}, u32[]{:S(2)}, u32[]{:S(2)}) %all-to-all-start.1) | async-done | bytes 1114144 | tf_op jit(solution)/shard_map/all_to_all | solution.py:218
  86.7 1.0 copy-done.4
  87.7 1.3 shard_map.120
  89.0 1.0 copy-done
  90.0 10.7 %all-to-all-start.2 = ((bf16[64,32,256]{2,1,0:T(8,128)(2,1)}), bf16[64,32,256]{2,1,0:T(8,128)(2,1)S(1)}, u32[]{:S(2)}, u32[]{:S(2)}) async-start(bf16[64,32,256]{2,1,0:T(8,128)(2,1)} %bitcast.45), calls=%async_computation.2 | async-start | bytes 2097152 | tf_op jit(solution)/shard_map/all_to_all | solution.py:228
  100.8 1.6 %shard_map.122 = (bf16[2,1536,128]{2,1,0:T(8,128)(2,1)}, bf16[2,1536,128]{2,1,0:T(8,128)(2,1)S(1)}) custom-call(s32[1]{0:T(128)} %bitcast.22.core_ref, bf16[8,240,256]{2,1,0:T(8,128)(2,1)S(1)} %bitcast.44, bf16[8,272,256]{2,1,0:T(8,128)(2,1)S(1)} %all-to-all-done.1.b_ref, bf16[256,256]{1,0:T(8,128)(2,1)S(1)} %get-tuple-element.16.pair_ref, ...), custom_call_target="tpu_custom_call" | custom-call | flops 402653184 | bytes 4194304 | tf_op jit(solution)/shard_map/pallas_call | solution.py:233
  102.4 0.9 copy-done.1
  103.3 1.9 %collective-permute-start.3 = (bf16[2,1536,128]{2,1,0:T(8,128)(2,1)}, bf16[2,1536,128]{2,1,0:T(8,128)(2,1)S(1)}, u32[]{:S(2)}, u32[]{:S(2)}) collective-permute-start(bf16[2,1536,128]{2,1,0:T(8,128)(2,1)} %get-tuple-element.19), channel_id=1, source_target_pairs={{0,1},{1,0},{2,3},{3,2},{4,5},{5,4},{6,7},{7,6},{8,9},{9,8},{10,11... | collective-permute-start | bytes 2359304 | tf_op jit(solution)/shard_map/ppermute | solution.py:240
  105.3 0.1 copy.69
  105.5 0.1 copy.68
  105.6 0.1 copy.62.target_ref
  105.7 1.9 %collective-permute-done.3 = bf16[2,1536,128]{2,1,0:T(8,128)(2,1)S(1)} collective-permute-done((bf16[2,1536,128]{2,1,0:T(8,128)(2,1)}, bf16[2,1536,128]{2,1,0:T(8,128)(2,1)S(1)}, u32[]{:S(2)}, u32[]{:S(2)}) %collective-permute-start.3) | collective-permute-done | bytes 786464 | tf_op jit(solution)/shard_map/ppermute | solution.py:240
  107.7 0.9 copy-done.7
  108.6 1.5 convert_add_fusion
  110.1 5.5 %collective-permute-start.4 = (bf16[1536,128]{1,0:T(8,128)(2,1)S(1)}, bf16[1536,128]{1,0:T(8,128)(2,1)S(1)}, u32[]{:S(2)}, u32[]{:S(2)}) collective-permute-start(bf16[1536,128]{1,0:T(8,128)(2,1)S(1)} %fusion.1), channel_id=1, source_target_pairs={{0,2},{2,0},{1,3},{3,1},{4,6},{6,4},{5,7},{7,5},{8,10},{10,8},{9,1... | collective-permute-start | bytes 1179656 | tf_op jit(solution)/shard_map/ppermute | solution.py:244
  115.6 10.5 %all-to-all-done.2.parts_ref = bf16[64,32,256]{2,1,0:T(8,128)(2,1)S(1)} async-done(((bf16[64,32,256]{2,1,0:T(8,128)(2,1)}), bf16[64,32,256]{2,1,0:T(8,128)(2,1)S(1)}, u32[]{:S(2)}, u32[]{:S(2)}) %all-to-all-start.2) | async-done | bytes 1048608 | tf_op jit(solution)/shard_map/all_to_all | solution.py:228
  126.2 0.4 shard_map.121
  126.6 0.8 copy.63
  127.3 9.1 %all-to-all-start.3 = ((bf16[256,1,128]{2,1,0:T(2,128)(2,1)}), bf16[256,1,128]{2,1,0:T(2,128)(2,1)S(1)}, u32[]{:S(2)}, u32[]{:S(2)}) async-start(bf16[256,1,128]{2,1,0:T(2,128)(2,1)} %copy.63), calls=%async_computation.3 | async-start | bytes 262144 | tf_op jit(solution)/shard_map/all_to_all | solution.py:251
  136.5 14.3 %all-to-all-done.3 = bf16[256,1,128]{2,1,0:T(2,128)(2,1)S(1)} async-done(((bf16[256,1,128]{2,1,0:T(2,128)(2,1)}), bf16[256,1,128]{2,1,0:T(2,128)(2,1)S(1)}, u32[]{:S(2)}, u32[]{:S(2)}) %all-to-all-start.3) | async-done | bytes 65568 | tf_op jit(solution)/shard_map/all_to_all | solution.py:251
  150.8 0.1 convert_element_type.75
  151.0 0.1 slice_reduce_fusion.1
  151.1 0.1 copy.64
  151.2 0.1 copy.65.scores_ref
  151.4 0.1 copy.67
  151.5 0.7 reshape.136
  152.2 0.7 fusion.5
  153.0 0.8 shard_map.123
  (39 shorter events, 1.0 us)
Async XLA Ops:
  0.6 30.8 %copy-start.8 = (s32[128,1,2]{0,2,1:T(2,128)S(1)}, s32[128,1,2]{0,2,1:T(2,128)}, u32[]{:S(2)}) copy-start(s32[128,1,2]{0,2,1:T(2,128)} %param.11) | copy-start | bytes 3076
  0.6 30.8 %copy-start.9 = (s32[128,1,2]{0,2,1:T(2,128)S(1)}, s32[128,1,2]{0,2,1:T(2,128)}, u32[]{:S(2)}) copy-start(s32[128,1,2]{0,2,1:T(2,128)} %param.10) | copy-start | bytes 3076
  0.7 30.8 %copy-start.10 = (bf16[128,1,2]{0,2,1:T(2,128)(2,1)S(1)}, bf16[128,1,2]{0,2,1:T(2,128)(2,1)}, u32[]{:S(2)}) copy-start(bf16[128,1,2]{0,2,1:T(2,128)(2,1)} %param.12) | copy-start | bytes 1540
  0.7 0.7 copy-start.5
  1.4 0.7 copy-start.6
  3.0 49.5 %all-to-all-start = ((bf16[256,8,128]{2,1,0:T(8,128)(2,1)}), bf16[256,8,128]{2,1,0:T(8,128)(2,1)S(1)}, u32[]{:S(2)}, u32[]{:S(2)}) async-start(bf16[256,8,128]{2,1,0:T(8,128)(2,1)} %bitcast.2), calls=%async_computation | async-start | bytes 1048576 | tf_op jit(solution)/shard_map/all_to_all | solution.py:189
  31.7 11.0 %collective-permute-start = (bf16[64,12]{1,0:T(8,128)(2,1)S(1)}, bf16[64,12]{1,0:T(8,128)(2,1)S(1)}, u32[]{:S(2)}, u32[]{:S(2)}) collective-permute-start(bf16[64,12]{1,0:T(8,128)(2,1)S(1)} %reshape.133), channel_id=1, source_target_pairs={{0,12},{4,0},{8,4},{12,8},{1,13},{5,1},{9,5},{13,9},{2,14},{6,2},{... | collective-permute-start | bytes 4616 | tf_op jit(solution)/shard_map/ppermute | solution.py:191
  38.1 6.9 %collective-permute-start.1 = (bf16[64,12]{1,0:T(8,128)(2,1)S(1)}, bf16[64,12]{1,0:T(8,128)(2,1)S(1)}, u32[]{:S(2)}, u32[]{:S(2)}) collective-permute-start(bf16[64,12]{1,0:T(8,128)(2,1)S(1)} %reshape.133), channel_id=1, source_target_pairs={{0,8},{4,12},{8,0},{12,4},{1,9},{5,13},{9,1},{13,5},{2,10},{6,14},... | collective-permute-start | bytes 4616 | tf_op jit(solution)/shard_map/ppermute | solution.py:191
  40.0 7.6 %collective-permute-start.2 = (bf16[64,12]{1,0:T(8,128)(2,1)S(1)}, bf16[64,12]{1,0:T(8,128)(2,1)S(1)}, u32[]{:S(2)}, u32[]{:S(2)}) collective-permute-start(bf16[64,12]{1,0:T(8,128)(2,1)S(1)} %reshape.133), channel_id=1, source_target_pairs={{0,4},{4,8},{8,12},{12,0},{1,5},{5,9},{9,13},{13,1},{2,6},{6,10},{... | collective-permute-start | bytes 4616 | tf_op jit(solution)/shard_map/ppermute | solution.py:191
  54.6 32.1 %copy-start.2 = (bf16[1,2048,128]{2,1,0:T(8,128)(2,1)S(1)}, bf16[1,2048,128]{2,1,0:T(8,128)(2,1)}, u32[]{:S(2)}) copy-start(bf16[1,2048,128]{2,1,0:T(8,128)(2,1)} %param.13) | copy-start | bytes 1572868
  54.6 32.1 %copy-start.3 = (bf16[1,2048,128]{2,1,0:T(8,128)(2,1)S(1)}, bf16[1,2048,128]{2,1,0:T(8,128)(2,1)}, u32[]{:S(2)}) copy-start(bf16[1,2048,128]{2,1,0:T(8,128)(2,1)} %param.14) | copy-start | bytes 1572868
  54.6 32.1 %all-to-all-start.1 = ((bf16[8,272,256]{2,1,0:T(8,128)(2,1)}), bf16[8,272,256]{2,1,0:T(8,128)(2,1)S(1)}, u32[]{:S(2)}, u32[]{:S(2)}) async-start(bf16[8,272,256]{2,1,0:T(8,128)(2,1)} %broadcast_in_dim.54), calls=%async_computation.1 | async-start | bytes 2228224 | tf_op jit(solution)/shard_map/all_to_all | solution.py:218
  86.7 1.0 copy-start.4
  89.0 1.0 copy-start
  90.0 36.2 %all-to-all-start.2 = ((bf16[64,32,256]{2,1,0:T(8,128)(2,1)}), bf16[64,32,256]{2,1,0:T(8,128)(2,1)S(1)}, u32[]{:S(2)}, u32[]{:S(2)}) async-start(bf16[64,32,256]{2,1,0:T(8,128)(2,1)} %bitcast.45), calls=%async_computation.2 | async-start | bytes 2097152 | tf_op jit(solution)/shard_map/all_to_all | solution.py:228
  102.4 0.9 copy-start.1
  103.3 4.4 %collective-permute-start.3 = (bf16[2,1536,128]{2,1,0:T(8,128)(2,1)}, bf16[2,1536,128]{2,1,0:T(8,128)(2,1)S(1)}, u32[]{:S(2)}, u32[]{:S(2)}) collective-permute-start(bf16[2,1536,128]{2,1,0:T(8,128)(2,1)} %get-tuple-element.19), channel_id=1, source_target_pairs={{0,1},{1,0},{2,3},{3,2},{4,5},{5,4},{6,7},{7,6},{8,9},{9,8},{10,11... | collective-permute-start | bytes 2359304 | tf_op jit(solution)/shard_map/ppermute | solution.py:240
  107.7 0.9 copy-start.7
  110.1 42.8 %collective-permute-start.4 = (bf16[1536,128]{1,0:T(8,128)(2,1)S(1)}, bf16[1536,128]{1,0:T(8,128)(2,1)S(1)}, u32[]{:S(2)}, u32[]{:S(2)}) collective-permute-start(bf16[1536,128]{1,0:T(8,128)(2,1)S(1)} %fusion.1), channel_id=1, source_target_pairs={{0,2},{2,0},{1,3},{3,1},{4,6},{6,4},{5,7},{7,5},{8,10},{10,8},{9,1... | collective-permute-start | bytes 1179656 | tf_op jit(solution)/shard_map/ppermute | solution.py:244
  127.3 23.5 %all-to-all-start.3 = ((bf16[256,1,128]{2,1,0:T(2,128)(2,1)}), bf16[256,1,128]{2,1,0:T(2,128)(2,1)S(1)}, u32[]{:S(2)}, u32[]{:S(2)}) async-start(bf16[256,1,128]{2,1,0:T(2,128)(2,1)} %copy.63), calls=%async_computation.3 | async-start | bytes 262144 | tf_op jit(solution)/shard_map/all_to_all | solution.py:251

commit v5 on v4

--- a/solution.py
+++ b/solution.py
@@ -73,7 +73,7 @@
         in_specs=[VMEM] * 2,
         out_specs=HBM,
         scratch_shapes=[pltpu.VMEM(shape, BF), pltpu.SemaphoreType.DMA((experts,))],
-        compiler_params=pltpu.CompilerParams(vmem_limit_bytes=40 << 20),
+        compiler_params=pltpu.CompilerParams(vmem_limit_bytes=60 << 20),
     )(own_x, own_y)
 
 
@@ -149,8 +149,8 @@
     out_ref[...] = total.astype(BF)
 
 
-def sum_kernel(scores_ref, kept_ref, far_ref, gate_ref, up_ref, down_ref):
-    del scores_ref
+def sum_kernel(sent_ref, kept_ref, far_ref, gate_ref, up_ref, down_ref):
+    del sent_ref
     quarter, units = gate_ref.shape[1:]
     total = (kept_ref[...] + far_ref[...].astype(F32)).astype(BF)
     gate_ref[0] = total[:quarter]
@@ -264,7 +264,7 @@
         sum_kernel,
         [((1, quarter, units), BF)] * 2 + [((1, units, quarter), BF)],
         [ANY] + [VMEM] * 2,
-    )(scores, kept, far)
+    )(returned, kept, far)
     return grad_gate, grad_up, grad_down, token_grad, prob_grad[:, None, :]
 
 

time: 154 us -> 153 us (level)
  local copies, waits for them, and re-layouts: 9.69 us -> 7.98 us
    unnamed x22 -> x16, local copies, waits for them, and re-layouts: 5.26 us -> 2.9 us
  transfers between devices with their start and end apart: 9 -> 9, of which waited for: 7 -> 7; matrix products, arithmetic and copies ran while one was open for 4% -> 3% of each run, Pallas kernels for 1% -> 2%
where the time goes in v5:
time: 153 us; the launch traced here: 152 us
  starting transfers between devices  70.4 us (46%)
  waiting for transfers between devices  37.3 us (24%)
  blocking collectives  26.3 us (17%)
  local copies, waits for them, and re-layouts  7.98 us (5%)
  Pallas kernels  5.8 us (4%)
  other arithmetic  2.84 us (2%)
    all_to_all x1, starting transfers between devices, shards(): got = lax.all_to_all(block, ('expert', 'fsdp'), 0, 0, tiled=True)  28.4 us
    all_gather x1, blocking collectives, shards(): a_full = lax.all_gather(a_cut, 'fsdp', axis=0, axis_index_groups=in_row)  26.3 us
    all_to_all x1, waiting for transfers between devices, shards(): home = lax.all_to_all(returned, ('expert', 'fsdp'), 0, 0, tiled=True)  13.6 us
    ppermute x3, starting transfers between devices, shards(): lax.ppermute(fields, 'expert', [(i, (i + d) % experts) for i in range(exp...  10.9 us
    all_to_all x1, starting transfers between devices, shards(): lax.all_to_all(dx.reshape(peers, feats, rows), 'fsdp', 0, 0, tiled=True)  10.7 us
    all_to_all x1, waiting for transfers between devices, shards(): lax.all_to_all(dx.reshape(peers, feats, rows), 'fsdp', 0, 0, tiled=True)  10.5 us
    all_to_all x1, starting transfers between devices, shards(): home = lax.all_to_all(returned, ('expert', 'fsdp'), 0, 0, tiled=True)  9.11 us
    ppermute x1, starting transfers between devices, shards(): far = lax.ppermute(away, 'dp', [(0, 2), (2, 0), (1, 3), (3, 1)])  5.48 us
  transfers between devices with their start and end apart: 9, of which 7 were waited for; matrix products, arithmetic and copies ran while one was open for 3% of the time, Pallas kernels for 2%

profile of v5, /device:TPU:2, one launch (start us, length us, event | category | flops | bytes accessed | tf_op | source)
XLA Modules:
  0.0 152.2 jit_solution(15726747595894781280)
XLA Ops:
  0.7 1.7 %shard_map.119 = bf16[4,64,8,128]{3,2,1,0:T(8,128)(2,1)} custom-call(bf16[2,2048]{1,0:T(2,128)(2,1)} %bitcast.62, bf16[2,2048]{1,0:T(2,128)(2,1)} %bitcast.63), custom_call_target="tpu_custom_call" | custom-call | tf_op jit(solution)/shard_map/pallas_call | solution.py:70
  2.4 28.4 %all-to-all-start = ((bf16[256,8,128]{2,1,0:T(8,128)(2,1)}), bf16[256,8,128]{2,1,0:T(8,128)(2,1)S(1)}, u32[]{:S(2)}, u32[]{:S(2)}) async-start(bf16[256,8,128]{2,1,0:T(8,128)(2,1)} %bitcast.54), calls=%async_computation | async-start | bytes 1048576 | tf_op jit(solution)/shard_map/all_to_all | solution.py:189
  30.8 0.1 copy.52
  30.9 0.1 reshape.133
  31.0 6.4 %collective-permute-start = (bf16[64,12]{1,0:T(8,128)(2,1)S(1)}, bf16[64,12]{1,0:T(8,128)(2,1)S(1)}, u32[]{:S(2)}, u32[]{:S(2)}) collective-permute-start(bf16[64,12]{1,0:T(8,128)(2,1)S(1)} %reshape.133), channel_id=1, source_target_pairs={{0,12},{4,0},{8,4},{12,8},{1,13},{5,1},{9,5},{13,9},{2,14},{6,2},{... | collective-permute-start | bytes 4616 | tf_op jit(solution)/shard_map/ppermute | solution.py:191
  37.4 1.9 %collective-permute-start.1 = (bf16[64,12]{1,0:T(8,128)(2,1)S(1)}, bf16[64,12]{1,0:T(8,128)(2,1)S(1)}, u32[]{:S(2)}, u32[]{:S(2)}) collective-permute-start(bf16[64,12]{1,0:T(8,128)(2,1)S(1)} %reshape.133), channel_id=1, source_target_pairs={{0,8},{4,12},{8,0},{12,4},{1,9},{5,13},{9,1},{13,5},{2,10},{6,14},... | collective-permute-start | bytes 4616 | tf_op jit(solution)/shard_map/ppermute | solution.py:191
  39.3 2.6 %collective-permute-start.2 = (bf16[64,12]{1,0:T(8,128)(2,1)S(1)}, bf16[64,12]{1,0:T(8,128)(2,1)S(1)}, u32[]{:S(2)}, u32[]{:S(2)}) collective-permute-start(bf16[64,12]{1,0:T(8,128)(2,1)S(1)} %reshape.133), channel_id=1, source_target_pairs={{0,4},{4,8},{8,12},{12,0},{1,5},{5,9},{9,13},{13,1},{2,6},{6,10},{... | collective-permute-start | bytes 4616 | tf_op jit(solution)/shard_map/ppermute | solution.py:191
  42.0 0.1 copy.53
  42.1 2.2 %collective-permute-done.1 = bf16[64,12]{1,0:T(8,128)(2,1)S(1)} collective-permute-done((bf16[64,12]{1,0:T(8,128)(2,1)S(1)}, bf16[64,12]{1,0:T(8,128)(2,1)S(1)}, u32[]{:S(2)}, u32[]{:S(2)}) %collective-permute-start.1) | collective-permute-done | bytes 1568 | tf_op jit(solution)/shard_map/ppermute | solution.py:191
  44.4 2.5 %collective-permute-done.2 = bf16[64,12]{1,0:T(8,128)(2,1)S(1)} collective-permute-done((bf16[64,12]{1,0:T(8,128)(2,1)S(1)}, bf16[64,12]{1,0:T(8,128)(2,1)S(1)}, u32[]{:S(2)}, u32[]{:S(2)}) %collective-permute-start.2) | collective-permute-done | bytes 1568 | tf_op jit(solution)/shard_map/ppermute | solution.py:191
  47.0 0.1 concatenate.10
  47.2 4.7 %all-to-all-done = bf16[256,8,128]{2,1,0:T(8,128)(2,1)S(1)} async-done(((bf16[256,8,128]{2,1,0:T(8,128)(2,1)}), bf16[256,8,128]{2,1,0:T(8,128)(2,1)S(1)}, u32[]{:S(2)}, u32[]{:S(2)}) %all-to-all-start) | async-done | bytes 524320 | tf_op jit(solution)/shard_map/all_to_all | solution.py:189
  51.9 0.3 copy.50
  52.2 0.3 fusion.4
  52.5 0.3 fusion.1
  52.8 1.1 broadcast_in_dim.54
  53.9 3.9 %all-to-all-start.1 = ((bf16[8,272,256]{2,1,0:T(8,128)(2,1)}), bf16[8,272,256]{2,1,0:T(8,128)(2,1)S(1)}, u32[]{:S(2)}, u32[]{:S(2)}) async-start(bf16[8,272,256]{2,1,0:T(8,128)(2,1)} %broadcast_in_dim.54), calls=%async_computation.1 | async-start | bytes 2228224 | tf_op jit(solution)/shard_map/all_to_all | solution.py:218
  57.8 0.1 select_reduce_fusion.1
  58.0 0.1 select_reduce_fusion
  58.2 26.3 %all-gather = bf16[1920,256]{1,0:T(8,128)(2,1)S(1)} all-gather(bf16[240,256]{1,0:T(8,128)(2,1)S(1)} %slice.100), channel_id=2, replica_groups={{0,16,32,48,64,80,96,112},{128,144,160,176,192,208,224,240},{256,272,28..., dimensions={0}, use_global_device_ids=true | all-gather | bytes 1105920 | tf_op jit(solution)/shard_map/all_gather | solution.py:219
  84.5 1.5 %all-to-all-done.1.b_ref = bf16[8,272,256]{2,1,0:T(8,128)(2,1)S(1)} async-done(((bf16[8,272,256]{2,1,0:T(8,128)(2,1)}), bf16[8,272,256]{2,1,0:T(8,128)(2,1)S(1)}, u32[]{:S(2)}, u32[]{:S(2)}) %all-to-all-start.1) | async-done | bytes 1114144 | tf_op jit(solution)/shard_map/all_to_all | solution.py:218
  86.0 1.0 copy-done.4
  87.0 1.3 shard_map.120
  88.3 1.0 copy-done
  89.3 10.7 %all-to-all-start.2 = ((bf16[64,32,256]{2,1,0:T(8,128)(2,1)}), bf16[64,32,256]{2,1,0:T(8,128)(2,1)S(1)}, u32[]{:S(2)}, u32[]{:S(2)}) async-start(bf16[64,32,256]{2,1,0:T(8,128)(2,1)} %bitcast.46), calls=%async_computation.2 | async-start | bytes 2097152 | tf_op jit(solution)/shard_map/all_to_all | solution.py:228
  100.1 1.6 %shard_map.122 = (bf16[2,1536,128]{2,1,0:T(8,128)(2,1)}, bf16[2,1536,128]{2,1,0:T(8,128)(2,1)S(1)}) custom-call(s32[1]{0:T(128)} %bitcast.19.core_ref, bf16[8,240,256]{2,1,0:T(8,128)(2,1)S(1)} %bitcast.45, bf16[8,272,256]{2,1,0:T(8,128)(2,1)S(1)} %all-to-all-done.1.b_ref, bf16[256,256]{1,0:T(8,128)(2,1)S(1)} %get-tuple-element.16.pair_ref, ...), custom_call_target="tpu_custom_call" | custom-call | flops 402653184 | bytes 4194304 | tf_op jit(solution)/shard_map/pallas_call | solution.py:233
  101.7 0.9 copy-done.1
  102.5 1.9 %collective-permute-start.3 = (bf16[2,1536,128]{2,1,0:T(8,128)(2,1)}, bf16[2,1536,128]{2,1,0:T(8,128)(2,1)S(1)}, u32[]{:S(2)}, u32[]{:S(2)}) collective-permute-start(bf16[2,1536,128]{2,1,0:T(8,128)(2,1)} %get-tuple-element.19), channel_id=1, source_target_pairs={{0,1},{1,0},{2,3},{3,2},{4,5},{5,4},{6,7},{7,6},{8,9},{9,8},{10,11... | collective-permute-start | bytes 2359304 | tf_op jit(solution)/shard_map/ppermute | solution.py:240
  104.6 2.4 %collective-permute-done.3 = bf16[2,1536,128]{2,1,0:T(8,128)(2,1)S(1)} collective-permute-done((bf16[2,1536,128]{2,1,0:T(8,128)(2,1)}, bf16[2,1536,128]{2,1,0:T(8,128)(2,1)S(1)}, u32[]{:S(2)}, u32[]{:S(2)}) %collective-permute-start.3) | collective-permute-done | bytes 786464 | tf_op jit(solution)/shard_map/ppermute | solution.py:240
  106.9 1.3 convert_add_fusion
  108.3 0.8 fusion.3
  109.1 5.5 %collective-permute-start.4 = (bf16[1536,128]{1,0:T(8,128)(2,1)}, bf16[1536,128]{1,0:T(8,128)(2,1)S(1)}, u32[]{:S(2)}, u32[]{:S(2)}) collective-permute-start(bf16[1536,128]{1,0:T(8,128)(2,1)} %fusion.3), channel_id=1, source_target_pairs={{0,2},{2,0},{1,3},{3,1},{4,6},{6,4},{5,7},{7,5},{8,10},{10,8},{9,1... | collective-permute-start | bytes 1179656 | tf_op jit(solution)/shard_map/ppermute | solution.py:244
  114.6 0.1 copy.66
  114.7 0.1 copy.65
  114.8 0.1 copy.61.target_ref
  115.0 10.5 %all-to-all-done.2.parts_ref = bf16[64,32,256]{2,1,0:T(8,128)(2,1)S(1)} async-done(((bf16[64,32,256]{2,1,0:T(8,128)(2,1)}), bf16[64,32,256]{2,1,0:T(8,128)(2,1)S(1)}, u32[]{:S(2)}, u32[]{:S(2)}) %all-to-all-start.2) | async-done | bytes 1048608 | tf_op jit(solution)/shard_map/all_to_all | solution.py:228
  125.5 0.4 shard_map.121.sent_ref
  125.9 0.7 copy.62
  126.6 9.1 %all-to-all-start.3 = ((bf16[256,1,128]{2,1,0:T(2,128)(2,1)}), bf16[256,1,128]{2,1,0:T(2,128)(2,1)S(1)}, u32[]{:S(2)}, u32[]{:S(2)}) async-start(bf16[256,1,128]{2,1,0:T(2,128)(2,1)} %copy.62), calls=%async_computation.3 | async-start | bytes 262144 | tf_op jit(solution)/shard_map/all_to_all | solution.py:251
  135.8 0.8 shard_map.123
  136.6 13.6 %all-to-all-done.3 = bf16[256,1,128]{2,1,0:T(2,128)(2,1)S(1)} async-done(((bf16[256,1,128]{2,1,0:T(2,128)(2,1)}), bf16[256,1,128]{2,1,0:T(2,128)(2,1)S(1)}, u32[]{:S(2)}, u32[]{:S(2)}) %all-to-all-start.3) | async-done | bytes 65568 | tf_op jit(solution)/shard_map/all_to_all | solution.py:251
  150.2 0.1 convert_element_type.75
  150.4 0.1 slice_reduce_fusion
  150.5 0.1 copy.63
  150.6 0.1 copy.64
  150.7 0.7 reshape.135
  151.4 0.1 copy.67
  151.5 0.7 fusion.9
  (31 shorter events, 0.6 us)
Async XLA Ops:
  0.6 30.1 %copy-start.6 = (s32[128,1,2]{0,2,1:T(2,128)S(1)}, s32[128,1,2]{0,2,1:T(2,128)}, u32[]{:S(2)}) copy-start(s32[128,1,2]{0,2,1:T(2,128)} %param.11) | copy-start | bytes 3076
  0.6 30.1 %copy-start.5 = (s32[128,1,2]{0,2,1:T(2,128)S(1)}, s32[128,1,2]{0,2,1:T(2,128)}, u32[]{:S(2)}) copy-start(s32[128,1,2]{0,2,1:T(2,128)} %param.10) | copy-start | bytes 3076
  0.7 30.1 %copy-start.7 = (bf16[128,1,2]{0,2,1:T(2,128)(2,1)S(1)}, bf16[128,1,2]{0,2,1:T(2,128)(2,1)}, u32[]{:S(2)}) copy-start(bf16[128,1,2]{0,2,1:T(2,128)(2,1)} %param.12) | copy-start | bytes 1540
  2.4 49.5 %all-to-all-start = ((bf16[256,8,128]{2,1,0:T(8,128)(2,1)}), bf16[256,8,128]{2,1,0:T(8,128)(2,1)S(1)}, u32[]{:S(2)}, u32[]{:S(2)}) async-start(bf16[256,8,128]{2,1,0:T(8,128)(2,1)} %bitcast.54), calls=%async_computation | async-start | bytes 1048576 | tf_op jit(solution)/shard_map/all_to_all | solution.py:189
  31.0 11.0 %collective-permute-start = (bf16[64,12]{1,0:T(8,128)(2,1)S(1)}, bf16[64,12]{1,0:T(8,128)(2,1)S(1)}, u32[]{:S(2)}, u32[]{:S(2)}) collective-permute-start(bf16[64,12]{1,0:T(8,128)(2,1)S(1)} %reshape.133), channel_id=1, source_target_pairs={{0,12},{4,0},{8,4},{12,8},{1,13},{5,1},{9,5},{13,9},{2,14},{6,2},{... | collective-permute-start | bytes 4616 | tf_op jit(solution)/shard_map/ppermute | solution.py:191
  37.4 6.9 %collective-permute-start.1 = (bf16[64,12]{1,0:T(8,128)(2,1)S(1)}, bf16[64,12]{1,0:T(8,128)(2,1)S(1)}, u32[]{:S(2)}, u32[]{:S(2)}) collective-permute-start(bf16[64,12]{1,0:T(8,128)(2,1)S(1)} %reshape.133), channel_id=1, source_target_pairs={{0,8},{4,12},{8,0},{12,4},{1,9},{5,13},{9,1},{13,5},{2,10},{6,14},... | collective-permute-start | bytes 4616 | tf_op jit(solution)/shard_map/ppermute | solution.py:191
  39.3 7.6 %collective-permute-start.2 = (bf16[64,12]{1,0:T(8,128)(2,1)S(1)}, bf16[64,12]{1,0:T(8,128)(2,1)S(1)}, u32[]{:S(2)}, u32[]{:S(2)}) collective-permute-start(bf16[64,12]{1,0:T(8,128)(2,1)S(1)} %reshape.133), channel_id=1, source_target_pairs={{0,4},{4,8},{8,12},{12,0},{1,5},{5,9},{9,13},{13,1},{2,6},{6,10},{... | collective-permute-start | bytes 4616 | tf_op jit(solution)/shard_map/ppermute | solution.py:191
  53.9 32.1 %copy-start.2 = (bf16[1,2048,128]{2,1,0:T(8,128)(2,1)S(1)}, bf16[1,2048,128]{2,1,0:T(8,128)(2,1)}, u32[]{:S(2)}) copy-start(bf16[1,2048,128]{2,1,0:T(8,128)(2,1)} %param.13) | copy-start | bytes 1572868
  53.9 32.1 %copy-start.3 = (bf16[1,2048,128]{2,1,0:T(8,128)(2,1)S(1)}, bf16[1,2048,128]{2,1,0:T(8,128)(2,1)}, u32[]{:S(2)}) copy-start(bf16[1,2048,128]{2,1,0:T(8,128)(2,1)} %param.14) | copy-start | bytes 1572868
  53.9 32.1 %all-to-all-start.1 = ((bf16[8,272,256]{2,1,0:T(8,128)(2,1)}), bf16[8,272,256]{2,1,0:T(8,128)(2,1)S(1)}, u32[]{:S(2)}, u32[]{:S(2)}) async-start(bf16[8,272,256]{2,1,0:T(8,128)(2,1)} %broadcast_in_dim.54), calls=%async_computation.1 | async-start | bytes 2228224 | tf_op jit(solution)/shard_map/all_to_all | solution.py:218
  86.0 1.0 copy-start.4
  88.3 1.0 copy-start
  89.3 36.2 %all-to-all-start.2 = ((bf16[64,32,256]{2,1,0:T(8,128)(2,1)}), bf16[64,32,256]{2,1,0:T(8,128)(2,1)S(1)}, u32[]{:S(2)}, u32[]{:S(2)}) async-start(bf16[64,32,256]{2,1,0:T(8,128)(2,1)} %bitcast.46), calls=%async_computation.2 | async-start | bytes 2097152 | tf_op jit(solution)/shard_map/all_to_all | solution.py:228
  101.7 0.9 copy-start.1
  102.5 4.4 %collective-permute-start.3 = (bf16[2,1536,128]{2,1,0:T(8,128)(2,1)}, bf16[2,1536,128]{2,1,0:T(8,128)(2,1)S(1)}, u32[]{:S(2)}, u32[]{:S(2)}) collective-permute-start(bf16[2,1536,128]{2,1,0:T(8,128)(2,1)} %get-tuple-element.19), channel_id=1, source_target_pairs={{0,1},{1,0},{2,3},{3,2},{4,5},{5,4},{6,7},{7,6},{8,9},{9,8},{10,11... | collective-permute-start | bytes 2359304 | tf_op jit(solution)/shard_map/ppermute | solution.py:240
  109.1 26.7 %collective-permute-start.4 = (bf16[1536,128]{1,0:T(8,128)(2,1)}, bf16[1536,128]{1,0:T(8,128)(2,1)S(1)}, u32[]{:S(2)}, u32[]{:S(2)}) collective-permute-start(bf16[1536,128]{1,0:T(8,128)(2,1)} %fusion.3), channel_id=1, source_target_pairs={{0,2},{2,0},{1,3},{3,1},{4,6},{6,4},{5,7},{7,5},{8,10},{10,8},{9,1... | collective-permute-start | bytes 1179656 | tf_op jit(solution)/shard_map/ppermute | solution.py:244
  126.6 23.6 %all-to-all-start.3 = ((bf16[256,1,128]{2,1,0:T(2,128)(2,1)}), bf16[256,1,128]{2,1,0:T(2,128)(2,1)S(1)}, u32[]{:S(2)}, u32[]{:S(2)}) async-start(bf16[256,1,128]{2,1,0:T(2,128)(2,1)} %copy.62), calls=%async_computation.3 | async-start | bytes 262144 | tf_op jit(solution)/shard_map/all_to_all | solution.py:251
